TPU v7x, 256 devices: a whole 4x4x8 slice. The times are simulated.
256 devices in a mesh: blk: 64 (over z, y, x_hi), tp: 4 (over x_lo, core).
Axes of the slice: x: 4 (x_hi: 2, x_lo: 2; x = x_hi * 2 + x_lo), y: 4, z: 8, core: 2. Of those that a mesh axis runs over, the one named last changes fastest.
Arguments:
- stream: bfloat16 [16384, 2560], P('blk', 'tp'), may hold values from -180 to 180, as said below
- norm_gain: bfloat16 [2560], P('tp'), may hold values from 0.099609375 to 1.8984375
- gate_weight: bfloat16 [2560, 7168], P('blk', 'tp'), may hold values from -0.125 to 0.125
- act_grad: bfloat16 [16384, 7168], P('blk', 'tp'), may hold values from -36 to 36
Outputs:
- gate_act: bfloat16 [16384, 7168], P('blk', 'tp')
- input_grad: bfloat16 [16384, 2560], P('blk', 'tp')
- weight_grad: float32 [2560, 7168], P('blk', 'tp')
- gain_grad: float32 [2560], P('tp')
Inputs may be any that keep to these rules, and one draw needn't show every extreme that they name: `stream`: token rows and feature columns carry independent scales.
All inputs are finite; a program needn't handle non-finite values.
Results may differ from a plain program's by a relative error of at most 0.015.
Values may be sent and summed in bfloat16 or wider, within the bound.
No kernel may reach another device: no remote copies, remote signals or barrier semaphores. Data moves between devices by JAX's collectives and lax.ppermute only.
A program may use at most 64 MiB of HBM per device.

v0:
```python
import jax
import jax.numpy as jnp
from jax import lax
from jax.experimental import pallas as pl
from jax.experimental.pallas import tpu as pltpu
from jax.sharding import Mesh, PartitionSpec as P

D = 2560
EPS = 1e-05
AXES = ("z", "y", "xh", "xl", "c")
SIZES = (8, 4, 2, 2, 2)
NUM = dict(zip(AXES, SIZES))
X = ("xh", "xl")
PART_A = 384
EXTRA = 16
BF = jnp.bfloat16
F32 = jnp.float32
VMEM_LIMIT = 32 * 1024 * 1024
NT = (((1,), (1,)), ((), ()))
TN = (((0,), (0,)), ((), ()))


def flip(a, axis, bit):
    names = axis if isinstance(axis, tuple) else (axis,)
    n = 1
    for name in names:
        n *= NUM[name]
    return lax.ppermute(a, axis, [(i, i ^ bit) for i in range(n)])


def together(*values):
    return lax.optimization_barrier(values)


def ring(a, d):
    n = NUM["z"]
    return lax.ppermute(a, "z", [(i, (i + d) % n) for i in range(n)])


def pair(index, mine, other, axis):
    first = index == 0
    return jnp.concatenate([jnp.where(first, mine, other), jnp.where(first, other, mine)], axis=axis)


def ordered(p, index):
    low, high = (index % 2) == 0, (index // 2) == 0
    p = [jnp.where(low, p[k], p[k ^ 1]) for k in range(4)]
    return [jnp.where(high, p[k], p[k ^ 2]) for k in range(4)]


def rows_at(a, block, size):
    return lax.dynamic_slice_in_dim(a, block * size, size, 0)


def norm_kernel(place, mine, other, normed, inv_ref, gain_ref):
    xl, c = place[0], place[1]
    tok = normed.shape[0]
    feat = mine.shape[-1]
    total = jnp.zeros((tok, 1), F32)
    for src in (mine, other):
        for dxl in (0, 1):
            v = src[0, dxl, :tok, :].astype(F32)
            total = total + jnp.sum(v * v, axis=1, keepdims=True)
    inv = lax.rsqrt(total / D + EPS)
    inv_ref[...] = inv
    for dc, src in enumerate((mine, other)):
        for dxl in (0, 1):
            at = pl.multiple_of(((xl ^ dxl) * 2 + (c ^ dc)) * feat, 128)
            gain = src[0, dxl, tok:, :].astype(F32)[:1]
            v = src[0, dxl, :tok, :].astype(F32)
            normed[:, pl.ds(at, feat)] = (v * inv * gain).astype(BF)
            gain_ref[:, pl.ds(at, feat)] = gain


def norm_call(place, mine, other):
    groups, _, rows, feat = mine.shape
    tok = rows - EXTRA
    block = pl.BlockSpec((1, 2, rows, feat), lambda i, s: (i, 0, 0, 0))
    return pl.pallas_call(
        norm_kernel,
        out_shape=(
            jax.ShapeDtypeStruct((groups * tok, D), BF),
            jax.ShapeDtypeStruct((groups * tok, 1), F32),
            jax.ShapeDtypeStruct((1, D), F32),
        ),
        grid_spec=pltpu.PrefetchScalarGridSpec(
            num_scalar_prefetch=1,
            grid=(groups,),
            in_specs=[block, block],
            out_specs=(
                pl.BlockSpec((tok, D), lambda i, s: (i, 0)),
                pl.BlockSpec((tok, 1), lambda i, s: (i, 0)),
                pl.BlockSpec((1, D), lambda i, s: (0, 0)),
            ),
        ),
        compiler_params=pltpu.CompilerParams(vmem_limit_bytes=VMEM_LIMIT),
        cost_estimate=pl.CostEstimate(flops=8 * tok * D, bytes_accessed=8 * tok * D, transcendentals=0),
        name="norm",
    )(place, mine, other)


def gate_kernel(start, normed, weight, cot, *refs):
    hid = weight.shape[1]
    pre = jnp.dot(normed[...], weight[...], preferred_element_type=F32)
    sig = 1.0 / (1.0 + jnp.exp(-pre))
    act = (pre * sig).astype(BF)
    grad = (cot[0, :, start:start + hid].astype(F32) * sig * (1.0 + pre * (1.0 - sig))).astype(BF)
    inner = jnp.sum(grad.astype(F32) * pre, axis=1, keepdims=True) / D
    if start:
        act_a, grad_a, inner_a = refs[:3]
        refs[3][0, :, :start] = act_a[0]
        refs[4][:, :start] = grad_a[...]
        inner = inner + inner_a[...]
    act_ref, grad_ref, inner_ref = refs[-3:]
    act_ref[0, :, start:start + hid] = act
    grad_ref[:, start:start + hid] = grad
    inner_ref[...] = inner


def gate_call(normed, weight, cot, start, *earlier):
    n, tok, width = cot.shape
    hid = weight.shape[1]
    col = pl.BlockSpec((tok, 1), lambda i: (i, 0))
    slab = lambda w: pl.BlockSpec((1, tok, w), lambda i: (i, 0, 0))
    rows = lambda w: pl.BlockSpec((tok, w), lambda i: (i, 0))
    return pl.pallas_call(
        lambda *refs: gate_kernel(start, *refs),
        out_shape=(
            jax.ShapeDtypeStruct((n, tok, start + hid), BF),
            jax.ShapeDtypeStruct((n * tok, start + hid), BF),
            jax.ShapeDtypeStruct((n * tok, 1), F32),
        ),
        grid=(n,),
        in_specs=[
            rows(D),
            pl.BlockSpec((D, hid), lambda i: (0, 0)),
            slab(width),
        ] + ([slab(start), rows(start), col] if start else []),
        out_specs=(slab(start + hid), rows(start + hid), col),
        compiler_params=pltpu.CompilerParams(vmem_limit_bytes=VMEM_LIMIT),
        cost_estimate=pl.CostEstimate(
            flops=2 * n * tok * D * hid, bytes_accessed=2 * D * (n * tok + hid), transcendentals=n * tok * hid
        ),
        name="gate",
    )(normed, weight, cot, *earlier)


def back_kernel(place, grad, weight_a, weight_b, normed, inner, gain, out_ref):
    part_a = weight_a.shape[1]
    part = lax.dot_general(grad[:, :part_a], weight_a[...], NT, preferred_element_type=F32)
    part = part + lax.dot_general(grad[:, part_a:], weight_b[...], NT, preferred_element_type=F32)
    rows = normed[...].astype(F32)
    g = gain[...]
    out = (part * g - rows * inner[...] * (1.0 / g)).astype(BF)
    terms = jnp.sum(part * rows, axis=0, keepdims=True).astype(BF)
    terms = jnp.broadcast_to(terms, (EXTRA, terms.shape[1]))
    groups, rows_out, _ = out_ref.shape
    tok = rows_out - EXTRA
    for i in range(groups):
        out_ref[i, :tok, :] = out[i * tok:(i + 1) * tok]
        out_ref[i, tok:, :] = terms


def back_call(place, grad, weight_a, weight_b, normed, inner, gain, dc, groups, feat):
    rows = grad.shape[0]
    tok = rows // groups
    which = lambda i, s: (s[0] ^ i) * 2 + (s[1] ^ dc)
    hid_a, hid_b = weight_a.shape[1], weight_b.shape[1]
    whole = lambda *shape: pl.BlockSpec(shape, lambda i, s: (0, 0))
    return pl.pallas_call(
        back_kernel,
        out_shape=jax.ShapeDtypeStruct((groups, tok + EXTRA, 2 * feat), BF),
        grid_spec=pltpu.PrefetchScalarGridSpec(
            num_scalar_prefetch=1,
            grid=(2,),
            in_specs=[
                whole(rows, hid_a + hid_b),
                pl.BlockSpec((feat, hid_a), lambda i, s: (which(i, s), 0)),
                pl.BlockSpec((feat, hid_b), lambda i, s: (which(i, s), 0)),
                pl.BlockSpec((rows, feat), lambda i, s: (0, which(i, s))),
                whole(rows, 1),
                pl.BlockSpec((1, feat), lambda i, s: (0, which(i, s))),
            ],
            out_specs=pl.BlockSpec((groups, tok + EXTRA, feat), lambda i, s: (0, 0, i)),
        ),
        compiler_params=pltpu.CompilerParams(vmem_limit_bytes=VMEM_LIMIT),
        cost_estimate=pl.CostEstimate(
            flops=2 * rows * D * (hid_a + hid_b) // 2, bytes_accessed=D * (3 * rows + hid_a + hid_b), transcendentals=0
        ),
        name="back",
    )(place, grad, weight_a, weight_b, normed, inner, gain)


def body(stream, norm_gain, gate_weight, act_grad):
    z, y, xh, xl, c = (lax.axis_index(a) for a in AXES)
    tok, feat = stream.shape
    hid = act_grad.shape[1] // 2
    wrows = gate_weight.shape[0]
    place = jnp.stack([xl, c]).astype(jnp.int32)
    scale = float(tok * 64) ** (-0.5)

    cut = lambda a, i: lax.dynamic_slice_in_dim(a, i * hid, hid, 1)
    w = pair(xh, cut(gate_weight, xh), flip(cut(gate_weight, 1 - xh), "xh", 1), 0)
    w_b = [w[:, PART_A:]]
    w_b = w_b + [flip(w_b[0], "y", k) for k in (1, 2, 3)]
    w_a = w[None, None, None, :, :PART_A]
    w_a = pair(z // 4, w_a, flip(w_a, "z", 4), 0)
    *w_b, stream = together(*w_b, stream)
    w_b = jnp.concatenate(ordered(w_b, y), axis=0)
    held = jnp.zeros((NUM["z"], *w_b.shape), BF)
    put = lambda held, block, i: lax.dynamic_update_index_in_dim(held, block, lax.rem(z + i, NUM["z"]), 0)
    held = put(held, w_b, 0)
    up = down = w_b
    for step in (1, 2, 3):
        up, down = ring(up, 1), ring(down, -1)
        if step == 1:
            up, down, act_grad = together(up, down, act_grad)
        held = put(put(held, up, NUM["z"] - step), down, step)
        if step < 3:
            w_a = pair((z // (4 >> step)) % 2, w_a, flip(w_a, "z", 4 >> step), step)
    last = ring(up, 1)
    weight_b = put(held, last, 4).reshape(D, hid - PART_A)
    w_a = w_a.reshape(NUM["z"], 2 * wrows, PART_A)

    payload = jnp.concatenate([stream, jnp.broadcast_to(norm_gain[None], (EXTRA, feat))], axis=0)
    near = jnp.stack([payload] + [flip(payload, X, m) for m in (1, 2, 3)])
    near = near.reshape(2, 2, tok + EXTRA, feat)
    normed, inv_all, gain = norm_call(place, near, flip(near, "c", 1))

    cot = jnp.stack([cut(act_grad, xh), flip(cut(act_grad, 1 - xh), "xh", 1)])

    w_a = [w_a] + [flip(w_a, "y", k) for k in (1, 2, 3)]
    *w_a, normed, cot = together(*w_a, normed, cot)
    weight_a = jnp.stack(ordered(w_a, y), axis=1).reshape(D, PART_A)

    act, grad, inner = gate_call(normed, weight_b, cot, PART_A, *gate_call(normed, weight_a, cot, 0))
    terms = lax.dot_general(normed, grad, TN, preferred_element_type=F32).astype(BF)
    terms, grad = together(terms, grad)
    sums_z = lax.psum_scatter(terms, "z", scatter_dimension=0, tiled=True)

    back = lambda dc: back_call(place, grad, weight_a, weight_b, normed, inner, gain, dc, 2, feat)
    first, second = back(1), back(0)
    sums = second.astype(F32) + flip(first, "c", 1).astype(F32)
    piece = lambda m: sums[m // 2, :, (m % 2) * feat:(m % 2 + 1) * feat].astype(BF)
    p = [piece(0).astype(F32)] + [flip(piece(m), X, m).astype(F32) for m in (1, 2, 3)]
    total = (p[0] + p[1]) + (p[2] + p[3])

    act, total = together(act, total)
    input_grad = (inv_all[:tok] * total[:tok]).astype(BF)
    gate_act = pair(xh, act[0], flip(act[1], "xh", 1), 1)

    gsum = sums[0, tok:tok + 1]
    for axis, bit in (("z", 1), ("z", 2), ("z", 4), ("y", 1), ("y", 2), ("xh", 1)):
        gsum = gsum + flip(gsum, axis, bit)
    gsum = gsum[:, :feat] + flip(gsum[:, feat:], "xl", 1)
    gain_grad = gsum[0] / norm_gain.astype(F32) * scale

    whole = rows_at(sums_z, y, 2 * wrows).astype(F32)
    for k in (1, 2, 3):
        whole = whole + flip(rows_at(sums_z, y ^ k, 2 * wrows), "y", k).astype(F32)
    other = flip(rows_at(whole, 1 - xh, wrows).astype(BF), "xh", 1).astype(F32)
    weight_grad = pair(xh, rows_at(whole, xh, wrows), other, 1) * scale
    return (gate_act, input_grad, weight_grad, gain_grad)


def solution(mesh):
    inner_mesh = Mesh(mesh.devices.reshape(SIZES), AXES)
    tokens, features = ("z", "y", "xh"), ("xl", "c")
    return jax.shard_map(
        body,
        mesh=inner_mesh,
        in_specs=(P(tokens, features), P(features), P(tokens, features), P(tokens, features)),
        out_specs=(P(tokens, features), P(tokens, features), P(tokens, features), P(features)),
        check_vma=False,
    )
```

profile of v0, /device:TPU:2, one launch (start us, length us, event | category | flops | bytes accessed | tf_op | source)
XLA Modules:
  0.0 176.1 jit_solution(16880325687234409852)
XLA Ops:
  8.1 2.1 %collective-permute-start = (bf16[40,896]{1,0:T(8,128)(2,1)S(1)}, bf16[40,896]{1,0:T(8,128)(2,1)S(1)}, u32[]{:S(2)}, u32[]{:S(2)}) collective-permute-start(bf16[40,896]{1,0:T(8,128)(2,1)S(1)} %constant_dynamic-slice_fusion.4), channel_id=1, source_target_pairs={{0,4},{4,0},{1,5},{5,1},{2,6},{6,2},{3,7},{7,3},{8,12},{12,8},{9,1... | collective-permute-start | bytes 215048 | tf_op jit(solution)/shard_map/ppermute | solution.py:28
  10.3 3.6 %collective-permute-done = bf16[40,896]{1,0:T(8,128)(2,1)S(1)} collective-permute-done((bf16[40,896]{1,0:T(8,128)(2,1)S(1)}, bf16[40,896]{1,0:T(8,128)(2,1)S(1)}, u32[]{:S(2)}, u32[]{:S(2)}) %collective-permute-start) | collective-permute-done | bytes 71712 | tf_op jit(solution)/shard_map/ppermute | solution.py:28
  14.9 7.3 %collective-permute-start.1 = (bf16[1,1,1,80,384]{4,3,2,1,0:T(8,128)(2,1)S(1)}, bf16[1,1,1,80,384]{4,3,2,1,0:T(8,128)(2,1)S(1)}, u32[]{:S(2)}, u32[]{:S(2)}) collective-permute-start(bf16[1,1,1,80,384]{4,3,2,1,0:T(8,128)(2,1)S(1)} %maximum_bitcast_fusion), channel_id=1, source_target_pairs={{0,128},{32,160},{64,192},{96,224},{128,0},{160,32},{192,64},{224,... | collective-permute-start | bytes 184328 | tf_op jit(solution)/shard_map/ppermute | solution.py:28
  22.2 3.0 %collective-permute-start.9 = (bf16[80,512]{1,0:T(8,128)(2,1)S(1)}, bf16[80,512]{1,0:T(8,128)(2,1)S(1)}, u32[]{:S(2)}, u32[]{:S(2)}) collective-permute-start(bf16[80,512]{1,0:T(8,128)(2,1)S(1)} %pad_maximum_fusion.9), channel_id=1, source_target_pairs={{0,24},{8,16},{16,8},{24,0},{1,25},{9,17},{17,9},{25,1},{2,26},{10... | collective-permute-start | bytes 245768 | tf_op jit(solution)/shard_map/ppermute | solution.py:28
  26.3 1.6 collective-permute-start.2
  28.7 2.4 %collective-permute-done.8 = bf16[80,512]{1,0:T(8,128)(2,1)S(1)} collective-permute-done((bf16[80,512]{1,0:T(8,128)(2,1)S(1)}, bf16[80,512]{1,0:T(8,128)(2,1)S(1)}, u32[]{:S(2)}, u32[]{:S(2)}) %collective-permute-start.8) | collective-permute-done | bytes 81952 | tf_op jit(solution)/shard_map/ppermute | solution.py:28
  31.4 1.9 %collective-permute-start.14 = (bf16[320,512]{1,0:T(8,128)(2,1)S(1)}, bf16[320,512]{1,0:T(8,128)(2,1)S(1)}, u32[]{:S(2)}, u32[]{:S(2)}) collective-permute-start(bf16[320,512]{1,0:T(8,128)(2,1)S(1)} %pad_maximum_fusion.6), channel_id=1, source_target_pairs={{0,32},{32,64},{64,96},{96,128},{128,160},{160,192},{192,224},{224... | collective-permute-start | bytes 983048 | tf_op jit(solution)/shard_map/ppermute | solution.py:37
  33.4 2.2 %collective-permute-start.11 = (bf16[272,640]{1,0:T(8,128)(2,1)S(1)}, bf16[272,640]{1,0:T(8,128)(2,1)S(1)}, u32[]{:S(2)}, u32[]{:S(2)}) collective-permute-start(bf16[272,640]{1,0:T(8,128)(2,1)S(1)} %get-tuple-element.79), channel_id=1, source_target_pairs={{0,4},{2,6},{4,0},{6,2},{1,5},{3,7},{5,1},{7,3},{8,12},{10,14},{12... | collective-permute-start | bytes 1044488 | tf_op jit(solution)/shard_map/ppermute | solution.py:28
  35.6 1.4 collective-permute-start.10
  39.2 1.9 %collective-permute-start.3 = (bf16[2,2,1,80,384]{4,3,2,1,0:T(8,128)(2,1)S(1)}, bf16[2,2,1,80,384]{4,3,2,1,0:T(8,128)(2,1)S(1)}, u32[]{:S(2)}, u32[]{:S(2)}) collective-permute-start(bf16[2,2,1,80,384]{4,3,2,1,0:T(8,128)(2,1)S(1)} %pad_maximum_fusion.7), channel_id=1, source_target_pairs={{0,32},{32,0},{64,96},{96,64},{128,160},{160,128},{192,224},{224,1... | collective-permute-start | bytes 737288 | tf_op jit(solution)/shard_map/ppermute | solution.py:28
  41.5 4.0 %collective-permute-done.11 = bf16[272,640]{1,0:T(8,128)(2,1)S(1)} collective-permute-done((bf16[272,640]{1,0:T(8,128)(2,1)S(1)}, bf16[272,640]{1,0:T(8,128)(2,1)S(1)}, u32[]{:S(2)}, u32[]{:S(2)}) %collective-permute-start.11) | collective-permute-done | bytes 348192 | tf_op jit(solution)/shard_map/ppermute | solution.py:28
  45.5 1.5 collective-permute-start.18
  47.0 3.2 %collective-permute-done.10 = bf16[272,640]{1,0:T(8,128)(2,1)S(1)} collective-permute-done((bf16[272,640]{1,0:T(8,128)(2,1)S(1)}, bf16[272,640]{1,0:T(8,128)(2,1)S(1)}, u32[]{:S(2)}, u32[]{:S(2)}) %collective-permute-start.10) | collective-permute-done | bytes 348192 | tf_op jit(solution)/shard_map/ppermute | solution.py:28
  50.7 1.5 collective-permute-start.6
  52.2 2.0 %collective-permute-start.19 = (bf16[320,512]{1,0:T(8,128)(2,1)S(1)}, bf16[320,512]{1,0:T(8,128)(2,1)S(1)}, u32[]{:S(2)}, u32[]{:S(2)}) collective-permute-start(bf16[320,512]{1,0:T(8,128)(2,1)S(1)} %collective-permute-done.17), channel_id=1, source_target_pairs={{0,32},{32,64},{64,96},{96,128},{128,160},{160,192},{192,224},{224... | collective-permute-start | bytes 983048 | tf_op jit(solution)/shard_map/ppermute | solution.py:37
  55.5 4.7 %collective-permute-done.16 = bf16[256,896]{1,0:T(8,128)(2,1)S(1)} collective-permute-done((bf16[256,896]{1,0:T(8,128)(2,1)S(1)}, bf16[256,896]{1,0:T(8,128)(2,1)S(1)}, u32[]{:S(2)}, u32[]{:S(2)}) %collective-permute-start.16) | collective-permute-done | bytes 458784 | tf_op jit(solution)/shard_map/ppermute | solution.py:28
  60.2 2.1 %collective-permute-start.5 = (bf16[8,80,384]{2,1,0:T(8,128)(2,1)S(1)}, bf16[8,80,384]{2,1,0:T(8,128)(2,1)S(1)}, u32[]{:S(2)}, u32[]{:S(2)}) collective-permute-start(bf16[8,80,384]{2,1,0:T(8,128)(2,1)S(1)} %bitcast.77), channel_id=1, source_target_pairs={{0,16},{8,24},{16,0},{24,8},{1,17},{9,25},{17,1},{25,9},{2,18},{10... | collective-permute-start | bytes 1474568 | tf_op jit(solution)/shard_map/ppermute | solution.py:28
  64.4 9.5 %collective-permute-done.21 = bf16[320,512]{1,0:T(8,128)(2,1)S(1)} collective-permute-done((bf16[320,512]{1,0:T(8,128)(2,1)S(1)}, bf16[320,512]{1,0:T(8,128)(2,1)S(1)}, u32[]{:S(2)}, u32[]{:S(2)}) %collective-permute-start.21) | collective-permute-done | bytes 327712 | tf_op jit(solution)/shard_map/ppermute | solution.py:37
  73.9 2.1 %norm.1 = (bf16[512,2560]{1,0:T(8,128)(2,1)S(1)}, f32[512,1]{1,0:T(8,128)S(1)}, f32[1,2560]{1,0:T(1,128)S(1)}) custom-call(s32[2]{0:T(128)S(1)} %pad_add_fusion.place, bf16[2,2,272,640]{3,2,1,0:T(8,128)(2,1)S(1)} %bitcast.75, bf16[2,2,272,640]{3,2,1,0:T(8,128)(2,1)S(1)} %collective-permute-done.13.other), custom_call_target="tpu_custom_call" | custom-call | flops 5242880 | bytes 5242880 | tf_op jit(solution)/shard_map/norm/pallas_call | solution.py:79
  76.2 3.7 %collective-permute-done.4 = bf16[8,80,384]{2,1,0:T(8,128)(2,1)S(1)} collective-permute-done((bf16[8,80,384]{2,1,0:T(8,128)(2,1)S(1)}, bf16[8,80,384]{2,1,0:T(8,128)(2,1)S(1)}, u32[]{:S(2)}, u32[]{:S(2)}) %collective-permute-start.4) | collective-permute-done | bytes 491552 | tf_op jit(solution)/shard_map/ppermute | solution.py:28
  80.4 2.2 %gate.2 = (bf16[2,256,384]{2,1,0:T(8,128)(2,1)S(1)}, bf16[512,384]{1,0:T(8,128)(2,1)S(1)}, f32[512,1]{1,0:T(8,128)S(1)}) custom-call(bf16[512,2560]{1,0:T(8,128)(2,1)S(1)} %get-tuple-element.38.refs_0_.normed, bf16[2560,384]{1,0:T(8,128)(2,1)S(1)} %bitcast.71, bf16[2,256,896]{2,1,0:T(8,128)(2,1)S(1)} %pad_maximum_fusion.2.refs_2_), custom_call_target="tpu_custom_call" | custom-call | flops 1006632960 | bytes 4587520 | tf_op jit(solution)/shard_map/gate/pallas_call | solution.py:126
  82.7 2.3 %gate.3 = (bf16[2,256,896]{2,1,0:T(8,128)(2,1)S(1)}, bf16[512,896]{1,0:T(8,128)(2,1)S(1)}, f32[512,1]{1,0:T(8,128)S(1)}) custom-call(bf16[512,2560]{1,0:T(8,128)(2,1)S(1)} %get-tuple-element.38.refs_0_.normed, bf16[2560,512]{1,0:T(8,128)(2,1)S(1)} %bitcast.68, bf16[2,256,896]{2,1,0:T(8,128)(2,1)S(1)} %pad_maximum_fusion.2.refs_2_, ...), custom_call_target="tpu_custom_call" | custom-call | flops 1342177280 | bytes 5242880 | tf_op jit(solution)/shard_map/gate/pallas_call | solution.py:126
  86.7 4.6 %convolution_convert_fusion = bf16[2560,896]{1,0:T(8,128)(2,1)} fusion(bf16[512,2560]{1,0:T(8,128)(2,1)S(1)} %get-tuple-element.38.refs_0_.normed, bf16[512,896]{1,0:T(8,128)(2,1)S(1)} %get-tuple-element.51.grad), kind=kOutput, calls=%fused_computation | convolution fusion | flops 2351104000 | bytes 8126464 | tf_op jit(solution)/shard_map/dot_general | solution.py:237
  91.3 1.7 copy-done.1
  93.0 1.5 copy-done.3
  95.5 3.0 %back.3 = bf16[2,272,1280]{2,1,0:T(8,128)(2,1)S(1)} custom-call(s32[2]{0:T(128)S(1)} %pad_add_fusion.place, bf16[512,896]{1,0:T(8,128)(2,1)S(1)} %get-tuple-element.51.grad, bf16[2560,384]{1,0:T(8,128)(2,1)S(1)} %bitcast.72, bf16[2560,512]{1,0:T(8,128)(2,1)S(1)} %bitcast.69, bf16[512,2560]{1,0:T(8,128)(2,1)S(1)} %get-tuple-element.38.refs_0_.normed, ...), custom_call_target="tpu_custom_call" | custom-call | flops 1174405120 | bytes 6225920 | tf_op jit(solution)/shard_map/back/pallas_call | solution.py:170
  98.6 3.0 %back.2 = bf16[2,272,1280]{2,1,0:T(8,128)(2,1)S(1)} custom-call(s32[2]{0:T(128)S(1)} %pad_add_fusion.place, bf16[512,896]{1,0:T(8,128)(2,1)S(1)} %get-tuple-element.51.grad, bf16[2560,384]{1,0:T(8,128)(2,1)S(1)} %bitcast.73, bf16[2560,512]{1,0:T(8,128)(2,1)S(1)} %bitcast.70, bf16[512,2560]{1,0:T(8,128)(2,1)S(1)} %get-tuple-element.38.refs_0_.normed, ...), custom_call_target="tpu_custom_call" | custom-call | flops 1174405120 | bytes 6225920 | tf_op jit(solution)/shard_map/back/pallas_call | solution.py:170
  103.2 2.5 %collective-permute-start.23 = (bf16[272,640]{1,0:T(8,128)(2,1)}, bf16[272,640]{1,0:T(8,128)(2,1)S(1)}, u32[]{:S(2)}, u32[]{:S(2)}) collective-permute-start(bf16[272,640]{1,0:T(8,128)(2,1)} %get-tuple-element.64), channel_id=1, source_target_pairs={{0,2},{2,0},{4,6},{6,4},{1,3},{3,1},{5,7},{7,5},{8,10},{10,8},{12,... | collective-permute-start | bytes 1044488 | tf_op jit(solution)/shard_map/ppermute | solution.py:28
  105.7 1.4 collective-permute-start.25
  107.8 3.3 %collective-permute-start.32 = (f32[1,1280]{1,0:T(1,128)S(1)}, f32[1,1280]{1,0:T(1,128)S(1)}, u32[]{:S(2)}, u32[]{:S(2)}) collective-permute-start(f32[1,1280]{1,0:T(1,128)S(1)} %fusion.2), channel_id=1, source_target_pairs={{0,64},{32,96},{64,0},{96,32},{128,192},{160,224},{192,128},{224,1... | collective-permute-start | bytes 15368 | tf_op jit(solution)/shard_map/ppermute | solution.py:28
  111.0 1.9 %collective-permute-done.32 = f32[1,1280]{1,0:T(1,128)S(1)} collective-permute-done((f32[1,1280]{1,0:T(1,128)S(1)}, f32[1,1280]{1,0:T(1,128)S(1)}, u32[]{:S(2)}, u32[]{:S(2)}) %collective-permute-start.32) | collective-permute-done | bytes 5152 | tf_op jit(solution)/shard_map/ppermute | solution.py:28
  112.9 2.5 %collective-permute-start.33 = (f32[1,1280]{1,0:T(1,128)S(1)}, f32[1,1280]{1,0:T(1,128)S(1)}, u32[]{:S(2)}, u32[]{:S(2)}) collective-permute-start(f32[1,1280]{1,0:T(1,128)S(1)} %add.165), channel_id=1, source_target_pairs={{0,128},{32,160},{64,192},{96,224},{128,0},{160,32},{192,64},{224,... | collective-permute-start | bytes 15368 | tf_op jit(solution)/shard_map/ppermute | solution.py:28
  115.4 5.4 %collective-permute-done.33 = f32[1,1280]{1,0:T(1,128)S(1)} collective-permute-done((f32[1,1280]{1,0:T(1,128)S(1)}, f32[1,1280]{1,0:T(1,128)S(1)}, u32[]{:S(2)}, u32[]{:S(2)}) %collective-permute-start.33) | collective-permute-done | bytes 5152 | tf_op jit(solution)/shard_map/ppermute | solution.py:28
  122.1 2.5 %collective-permute-done.34 = f32[1,1280]{1,0:T(1,128)S(1)} collective-permute-done((f32[1,1280]{1,0:T(1,128)S(1)}, f32[1,1280]{1,0:T(1,128)S(1)}, u32[]{:S(2)}, u32[]{:S(2)}) %collective-permute-start.34) | collective-permute-done | bytes 5152 | tf_op jit(solution)/shard_map/ppermute | solution.py:28
  124.5 1.6 collective-permute-start.35
  126.2 3.6 %collective-permute-done.35 = f32[1,1280]{1,0:T(1,128)S(1)} collective-permute-done((f32[1,1280]{1,0:T(1,128)S(1)}, f32[1,1280]{1,0:T(1,128)S(1)}, u32[]{:S(2)}, u32[]{:S(2)}) %collective-permute-start.35) | collective-permute-done | bytes 5152 | tf_op jit(solution)/shard_map/ppermute | solution.py:28
  129.7 2.7 %collective-permute-start.36 = (f32[1,1280]{1,0:T(1,128)S(1)}, f32[1,1280]{1,0:T(1,128)S(1)}, u32[]{:S(2)}, u32[]{:S(2)}) collective-permute-start(f32[1,1280]{1,0:T(1,128)S(1)} %add.168), channel_id=1, source_target_pairs={{0,4},{4,0},{1,5},{5,1},{2,6},{6,2},{3,7},{7,3},{8,12},{12,8},{9,1... | collective-permute-start | bytes 15368 | tf_op jit(solution)/shard_map/ppermute | solution.py:28
  132.4 2.5 %collective-permute-done.36 = f32[1,1280]{1,0:T(1,128)S(1)} collective-permute-done((f32[1,1280]{1,0:T(1,128)S(1)}, f32[1,1280]{1,0:T(1,128)S(1)}, u32[]{:S(2)}, u32[]{:S(2)}) %collective-permute-start.36) | collective-permute-done | bytes 5152 | tf_op jit(solution)/shard_map/ppermute | solution.py:28
  135.0 1.9 %collective-permute-start.37 = (f32[1,640]{1,0:T(1,128)S(1)}, f32[1,640]{1,0:T(1,128)S(1)}, u32[]{:S(2)}, u32[]{:S(2)}) collective-permute-start(f32[1,640]{1,0:T(1,128)S(1)} %slice.62), channel_id=1, source_target_pairs={{0,2},{2,0},{1,3},{3,1},{4,6},{6,4},{5,7},{7,5},{8,10},{10,8},{9,1... | collective-permute-start | bytes 7688 | tf_op jit(solution)/shard_map/ppermute | solution.py:28
  137.0 1.7 collective-permute-done.37
  138.7 1.3 fusion
  140.0 2.8 %collective-permute-start.26 = (bf16[256,896]{1,0:T(8,128)(2,1)S(1)}, bf16[256,896]{1,0:T(8,128)(2,1)S(1)}, u32[]{:S(2)}, u32[]{:S(2)}) collective-permute-start(bf16[256,896]{1,0:T(8,128)(2,1)S(1)} %slice_bitcast_fusion), channel_id=1, source_target_pairs={{0,4},{4,0},{1,5},{5,1},{2,6},{6,2},{3,7},{7,3},{8,12},{12,8},{9,1... | collective-permute-start | bytes 1376264 | tf_op jit(solution)/shard_map/ppermute | solution.py:28
  144.2 5.2 %reduce-scatter.2.cloned.1.call-done = bf16[320,896]{1,0:T(8,128)(2,1)} async-done(((bf16[2560,896]{1,0:T(8,128)(2,1)}), bf16[320,896]{1,0:T(8,128)(2,1)}) %reduce-scatter.2.cloned.1.call-update) | async-done | bytes 573456 | tf_op jit(solution)/shard_map/reduce_scatter | solution.py:239
  150.5 1.6 collective-permute-start.27
  152.0 2.1 %collective-permute-start.29 = (bf16[80,896]{1,0:T(8,128)(2,1)S(1)}, bf16[80,896]{1,0:T(8,128)(2,1)S(1)}, u32[]{:S(2)}, u32[]{:S(2)}) collective-permute-start(bf16[80,896]{1,0:T(8,128)(2,1)S(1)} %get-tuple-element.72), channel_id=1, source_target_pairs={{0,24},{8,16},{16,8},{24,0},{1,25},{9,17},{17,9},{25,1},{2,26},{10... | collective-permute-start | bytes 430088 | tf_op jit(solution)/shard_map/ppermute | solution.py:28
  156.1 5.5 %collective-permute-done.29 = bf16[80,896]{1,0:T(8,128)(2,1)S(1)} collective-permute-done((bf16[80,896]{1,0:T(8,128)(2,1)S(1)}, bf16[80,896]{1,0:T(8,128)(2,1)S(1)}, u32[]{:S(2)}, u32[]{:S(2)}) %collective-permute-start.29) | collective-permute-done | bytes 143392 | tf_op jit(solution)/shard_map/ppermute | solution.py:28
  162.6 2.2 %collective-permute-start.30 = (bf16[40,896]{1,0:T(8,128)(2,1)S(1)}, bf16[40,896]{1,0:T(8,128)(2,1)S(1)}, u32[]{:S(2)}, u32[]{:S(2)}) collective-permute-start(bf16[40,896]{1,0:T(8,128)(2,1)S(1)} %dynamic-slice_convert_fusion), channel_id=1, source_target_pairs={{0,4},{4,0},{1,5},{5,1},{2,6},{6,2},{3,7},{7,3},{8,12},{12,8},{9,1... | collective-permute-start | bytes 215048 | tf_op jit(solution)/shard_map/ppermute | solution.py:28
  165.8 2.8 %collective-permute-done.30 = bf16[40,896]{1,0:T(8,128)(2,1)S(1)} collective-permute-done((bf16[40,896]{1,0:T(8,128)(2,1)S(1)}, bf16[40,896]{1,0:T(8,128)(2,1)S(1)}, u32[]{:S(2)}, u32[]{:S(2)}) %collective-permute-start.30) | collective-permute-done | bytes 71712 | tf_op jit(solution)/shard_map/ppermute | solution.py:28
  (119 shorter events, 24.8 us)
Async XLA Ops:
  7.2 26.2 %copy-start.12 = (bf16[256,640]{1,0:T(8,128)(2,1)S(1)}, bf16[256,640]{1,0:T(8,128)(2,1)}, u32[]{:S(2)}) copy-start(bf16[256,640]{1,0:T(8,128)(2,1)} %param.4) | copy-start | bytes 983044
  7.2 26.2 %copy-start.13 = (bf16[640]{0:T(1024)(128)(2,1)S(1)}, bf16[640]{0:T(1024)(128)(2,1)}, u32[]{:S(2)}) copy-start(bf16[640]{0:T(1024)(128)(2,1)} %param.5) | copy-start | bytes 3844
  7.2 142.2 %reduce-scatter.2.cloned.1.call-start = ((), (), s32[]{:S(2)}) async-start(), calls=%async_computation.1 | async-start | bytes 5160960 | tf_op jit(solution)/shard_map/reduce_scatter | solution.py:239
  8.1 5.8 %collective-permute-start = (bf16[40,896]{1,0:T(8,128)(2,1)S(1)}, bf16[40,896]{1,0:T(8,128)(2,1)S(1)}, u32[]{:S(2)}, u32[]{:S(2)}) collective-permute-start(bf16[40,896]{1,0:T(8,128)(2,1)S(1)} %constant_dynamic-slice_fusion.4), channel_id=1, source_target_pairs={{0,4},{4,0},{1,5},{5,1},{2,6},{6,2},{3,7},{7,3},{8,12},{12,8},{9,1... | collective-permute-start | bytes 215048 | tf_op jit(solution)/shard_map/ppermute | solution.py:28
  14.9 11.4 %collective-permute-start.1 = (bf16[1,1,1,80,384]{4,3,2,1,0:T(8,128)(2,1)S(1)}, bf16[1,1,1,80,384]{4,3,2,1,0:T(8,128)(2,1)S(1)}, u32[]{:S(2)}, u32[]{:S(2)}) collective-permute-start(bf16[1,1,1,80,384]{4,3,2,1,0:T(8,128)(2,1)S(1)} %maximum_bitcast_fusion), channel_id=1, source_target_pairs={{0,128},{32,160},{64,192},{96,224},{128,0},{160,32},{192,64},{224,... | collective-permute-start | bytes 184328 | tf_op jit(solution)/shard_map/ppermute | solution.py:28
  22.2 6.5 %collective-permute-start.9 = (bf16[80,512]{1,0:T(8,128)(2,1)S(1)}, bf16[80,512]{1,0:T(8,128)(2,1)S(1)}, u32[]{:S(2)}, u32[]{:S(2)}) collective-permute-start(bf16[80,512]{1,0:T(8,128)(2,1)S(1)} %pad_maximum_fusion.9), channel_id=1, source_target_pairs={{0,24},{8,16},{16,8},{24,0},{1,25},{9,17},{17,9},{25,1},{2,26},{10... | collective-permute-start | bytes 245768 | tf_op jit(solution)/shard_map/ppermute | solution.py:28
  25.2 5.9 %collective-permute-start.8 = (bf16[80,512]{1,0:T(8,128)(2,1)S(1)}, bf16[80,512]{1,0:T(8,128)(2,1)S(1)}, u32[]{:S(2)}, u32[]{:S(2)}) collective-permute-start(bf16[80,512]{1,0:T(8,128)(2,1)S(1)} %pad_maximum_fusion.9), channel_id=1, source_target_pairs={{0,16},{8,24},{16,0},{24,8},{1,17},{9,25},{17,1},{25,9},{2,18},{10... | collective-permute-start | bytes 245768 | tf_op jit(solution)/shard_map/ppermute | solution.py:28
  25.8 5.3 %collective-permute-start.7 = (bf16[80,512]{1,0:T(8,128)(2,1)S(1)}, bf16[80,512]{1,0:T(8,128)(2,1)S(1)}, u32[]{:S(2)}, u32[]{:S(2)}) collective-permute-start(bf16[80,512]{1,0:T(8,128)(2,1)S(1)} %pad_maximum_fusion.9), channel_id=1, source_target_pairs={{0,8},{8,0},{16,24},{24,16},{1,9},{9,1},{17,25},{25,17},{2,10},{10... | collective-permute-start | bytes 245768 | tf_op jit(solution)/shard_map/ppermute | solution.py:28
  26.3 11.0 %collective-permute-start.2 = (bf16[2,1,1,80,384]{4,3,2,1,0:T(8,128)(2,1)S(1)}, bf16[2,1,1,80,384]{4,3,2,1,0:T(8,128)(2,1)S(1)}, u32[]{:S(2)}, u32[]{:S(2)}) collective-permute-start(bf16[2,1,1,80,384]{4,3,2,1,0:T(8,128)(2,1)S(1)} %pad_maximum_fusion.8), channel_id=1, source_target_pairs={{0,64},{32,96},{64,0},{96,32},{128,192},{160,224},{192,128},{224,1... | collective-permute-start | bytes 368648 | tf_op jit(solution)/shard_map/ppermute | solution.py:28
  31.2 8.0 %collective-permute-start.15 = (bf16[320,512]{1,0:T(8,128)(2,1)S(1)}, bf16[320,512]{1,0:T(8,128)(2,1)S(1)}, u32[]{:S(2)}, u32[]{:S(2)}) collective-permute-start(bf16[320,512]{1,0:T(8,128)(2,1)S(1)} %pad_maximum_fusion.6), channel_id=1, source_target_pairs={{0,224},{32,0},{64,32},{96,64},{128,96},{160,128},{192,160},{224,1... | collective-permute-start | bytes 983048 | tf_op jit(solution)/shard_map/ppermute | solution.py:37
  31.4 9.7 %collective-permute-start.14 = (bf16[320,512]{1,0:T(8,128)(2,1)S(1)}, bf16[320,512]{1,0:T(8,128)(2,1)S(1)}, u32[]{:S(2)}, u32[]{:S(2)}) collective-permute-start(bf16[320,512]{1,0:T(8,128)(2,1)S(1)} %pad_maximum_fusion.6), channel_id=1, source_target_pairs={{0,32},{32,64},{64,96},{96,128},{128,160},{160,192},{192,224},{224... | collective-permute-start | bytes 983048 | tf_op jit(solution)/shard_map/ppermute | solution.py:37
  33.4 7.9 %copy-start.11 = (bf16[256,1792]{1,0:T(8,128)(2,1)S(1)}, bf16[256,1792]{1,0:T(8,128)(2,1)}, u32[]{:S(2)}) copy-start(bf16[256,1792]{1,0:T(8,128)(2,1)} %param.7) | copy-start | bytes 2752516
  33.4 12.0 %collective-permute-start.11 = (bf16[272,640]{1,0:T(8,128)(2,1)S(1)}, bf16[272,640]{1,0:T(8,128)(2,1)S(1)}, u32[]{:S(2)}, u32[]{:S(2)}) collective-permute-start(bf16[272,640]{1,0:T(8,128)(2,1)S(1)} %get-tuple-element.79), channel_id=1, source_target_pairs={{0,4},{2,6},{4,0},{6,2},{1,5},{3,7},{5,1},{7,3},{8,12},{10,14},{12... | collective-permute-start | bytes 1044488 | tf_op jit(solution)/shard_map/ppermute | solution.py:28
  35.6 14.6 %collective-permute-start.10 = (bf16[272,640]{1,0:T(8,128)(2,1)S(1)}, bf16[272,640]{1,0:T(8,128)(2,1)S(1)}, u32[]{:S(2)}, u32[]{:S(2)}) collective-permute-start(bf16[272,640]{1,0:T(8,128)(2,1)S(1)} %get-tuple-element.79), channel_id=1, source_target_pairs={{0,2},{2,0},{4,6},{6,4},{1,3},{3,1},{5,7},{7,5},{8,10},{10,8},{12,... | collective-permute-start | bytes 1044488 | tf_op jit(solution)/shard_map/ppermute | solution.py:28
  37.3 12.9 %collective-permute-start.12 = (bf16[272,640]{1,0:T(8,128)(2,1)S(1)}, bf16[272,640]{1,0:T(8,128)(2,1)S(1)}, u32[]{:S(2)}, u32[]{:S(2)}) collective-permute-start(bf16[272,640]{1,0:T(8,128)(2,1)S(1)} %get-tuple-element.79), channel_id=1, source_target_pairs={{0,6},{2,4},{4,2},{6,0},{1,7},{3,5},{5,3},{7,1},{8,14},{10,12},{12... | collective-permute-start | bytes 1044488 | tf_op jit(solution)/shard_map/ppermute | solution.py:28
  39.2 11.3 %collective-permute-start.3 = (bf16[2,2,1,80,384]{4,3,2,1,0:T(8,128)(2,1)S(1)}, bf16[2,2,1,80,384]{4,3,2,1,0:T(8,128)(2,1)S(1)}, u32[]{:S(2)}, u32[]{:S(2)}) collective-permute-start(bf16[2,2,1,80,384]{4,3,2,1,0:T(8,128)(2,1)S(1)} %pad_maximum_fusion.7), channel_id=1, source_target_pairs={{0,32},{32,0},{64,96},{96,64},{128,160},{160,128},{192,224},{224,1... | collective-permute-start | bytes 737288 | tf_op jit(solution)/shard_map/ppermute | solution.py:28
  41.1 11.1 %collective-permute-start.17 = (bf16[320,512]{1,0:T(8,128)(2,1)S(1)}, bf16[320,512]{1,0:T(8,128)(2,1)S(1)}, u32[]{:S(2)}, u32[]{:S(2)}) collective-permute-start(bf16[320,512]{1,0:T(8,128)(2,1)S(1)} %collective-permute-done.14), channel_id=1, source_target_pairs={{0,32},{32,64},{64,96},{96,128},{128,160},{160,192},{192,224},{224... | collective-permute-start | bytes 983048 | tf_op jit(solution)/shard_map/ppermute | solution.py:37
  45.5 8.8 %collective-permute-start.18 = (bf16[320,512]{1,0:T(8,128)(2,1)S(1)}, bf16[320,512]{1,0:T(8,128)(2,1)S(1)}, u32[]{:S(2)}, u32[]{:S(2)}) collective-permute-start(bf16[320,512]{1,0:T(8,128)(2,1)S(1)} %collective-permute-done.15), channel_id=1, source_target_pairs={{0,224},{32,0},{64,32},{96,64},{128,96},{160,128},{192,160},{224,1... | collective-permute-start | bytes 983048 | tf_op jit(solution)/shard_map/ppermute | solution.py:37
  50.2 10.0 %collective-permute-start.16 = (bf16[256,896]{1,0:T(8,128)(2,1)S(1)}, bf16[256,896]{1,0:T(8,128)(2,1)S(1)}, u32[]{:S(2)}, u32[]{:S(2)}) collective-permute-start(bf16[256,896]{1,0:T(8,128)(2,1)S(1)} %get-tuple-element.70), channel_id=1, source_target_pairs={{0,4},{4,0},{1,5},{5,1},{2,6},{6,2},{3,7},{7,3},{8,12},{12,8},{9,1... | collective-permute-start | bytes 1376264 | tf_op jit(solution)/shard_map/ppermute | solution.py:28
  50.5 23.4 %collective-permute-start.13 = (bf16[2,2,272,640]{3,2,1,0:T(8,128)(2,1)S(1)}, bf16[2,2,272,640]{3,2,1,0:T(8,128)(2,1)S(1)}, u32[]{:S(2)}, u32[]{:S(2)}) collective-permute-start(bf16[2,2,272,640]{3,2,1,0:T(8,128)(2,1)S(1)} %bitcast.74), channel_id=1, source_target_pairs={{0,1},{1,0},{2,3},{3,2},{4,5},{5,4},{6,7},{7,6},{8,9},{9,8},{10,11... | collective-permute-start | bytes 4177928 | tf_op jit(solution)/shard_map/ppermute | solution.py:28
  50.7 25.4 %collective-permute-start.6 = (bf16[8,80,384]{2,1,0:T(8,128)(2,1)S(1)}, bf16[8,80,384]{2,1,0:T(8,128)(2,1)S(1)}, u32[]{:S(2)}, u32[]{:S(2)}) collective-permute-start(bf16[8,80,384]{2,1,0:T(8,128)(2,1)S(1)} %bitcast.76), channel_id=1, source_target_pairs={{0,24},{8,16},{16,8},{24,0},{1,25},{9,17},{17,9},{25,1},{2,26},{10... | collective-permute-start | bytes 1474568 | tf_op jit(solution)/shard_map/ppermute | solution.py:28
  52.2 11.0 %collective-permute-start.19 = (bf16[320,512]{1,0:T(8,128)(2,1)S(1)}, bf16[320,512]{1,0:T(8,128)(2,1)S(1)}, u32[]{:S(2)}, u32[]{:S(2)}) collective-permute-start(bf16[320,512]{1,0:T(8,128)(2,1)S(1)} %collective-permute-done.17), channel_id=1, source_target_pairs={{0,32},{32,64},{64,96},{96,128},{128,160},{160,192},{192,224},{224... | collective-permute-start | bytes 983048 | tf_op jit(solution)/shard_map/ppermute | solution.py:37
  54.2 9.7 %collective-permute-start.20 = (bf16[320,512]{1,0:T(8,128)(2,1)S(1)}, bf16[320,512]{1,0:T(8,128)(2,1)S(1)}, u32[]{:S(2)}, u32[]{:S(2)}) collective-permute-start(bf16[320,512]{1,0:T(8,128)(2,1)S(1)} %collective-permute-done.18), channel_id=1, source_target_pairs={{0,224},{32,0},{64,32},{96,64},{128,96},{160,128},{192,160},{224,1... | collective-permute-start | bytes 983048 | tf_op jit(solution)/shard_map/ppermute | solution.py:37
  60.2 15.9 %collective-permute-start.5 = (bf16[8,80,384]{2,1,0:T(8,128)(2,1)S(1)}, bf16[8,80,384]{2,1,0:T(8,128)(2,1)S(1)}, u32[]{:S(2)}, u32[]{:S(2)}) collective-permute-start(bf16[8,80,384]{2,1,0:T(8,128)(2,1)S(1)} %bitcast.77), channel_id=1, source_target_pairs={{0,16},{8,24},{16,0},{24,8},{1,17},{9,25},{17,1},{25,9},{2,18},{10... | collective-permute-start | bytes 1474568 | tf_op jit(solution)/shard_map/ppermute | solution.py:28
  63.3 16.6 %collective-permute-start.4 = (bf16[8,80,384]{2,1,0:T(8,128)(2,1)S(1)}, bf16[8,80,384]{2,1,0:T(8,128)(2,1)S(1)}, u32[]{:S(2)}, u32[]{:S(2)}) collective-permute-start(bf16[8,80,384]{2,1,0:T(8,128)(2,1)S(1)} %bitcast.78), channel_id=1, source_target_pairs={{0,8},{8,0},{16,24},{24,16},{1,9},{9,1},{17,25},{25,17},{2,10},{10... | collective-permute-start | bytes 1474568 | tf_op jit(solution)/shard_map/ppermute | solution.py:28
  63.9 9.9 %collective-permute-start.21 = (bf16[320,512]{1,0:T(8,128)(2,1)S(1)}, bf16[320,512]{1,0:T(8,128)(2,1)S(1)}, u32[]{:S(2)}, u32[]{:S(2)}) collective-permute-start(bf16[320,512]{1,0:T(8,128)(2,1)S(1)} %collective-permute-done.19), channel_id=1, source_target_pairs={{0,32},{32,64},{64,96},{96,128},{128,160},{160,192},{192,224},{224... | collective-permute-start | bytes 983048 | tf_op jit(solution)/shard_map/ppermute | solution.py:37
  73.9 8.8 %copy-start = (bf16[8,320,512]{2,1,0:T(8,128)(2,1)}, bf16[8,320,512]{2,1,0:T(8,128)(2,1)S(1)}, u32[]{:S(2)}) copy-start(bf16[8,320,512]{2,1,0:T(8,128)(2,1)S(1)} %bitcast_dynamic-update-slice_fusion) | copy-start | bytes 7864324
  75.9 4.5 %copy-start.9 = (f32[512,1]{1,0:T(8,128)}, f32[512,1]{1,0:T(8,128)S(1)}, u32[]{:S(2)}) copy-start(f32[512,1]{1,0:T(8,128)S(1)} %get-tuple-element.55) | copy-start | bytes 6148
  95.5 3.1 %copy-start.6 = (f32[512,1]{1,0:T(8,128)S(1)}, f32[512,1]{1,0:T(8,128)}, u32[]{:S(2)}) copy-start(f32[512,1]{1,0:T(8,128)} %copy-done.4) | copy-start | bytes 6148
  98.5 3.2 %collective-permute-start.22 = (bf16[2,272,1280]{2,1,0:T(8,128)(2,1)S(1)}, bf16[2,272,1280]{2,1,0:T(8,128)(2,1)S(1)}, u32[]{:S(2)}, u32[]{:S(2)}) collective-permute-start(bf16[2,272,1280]{2,1,0:T(8,128)(2,1)S(1)} %back.3), channel_id=1, source_target_pairs={{0,1},{1,0},{2,3},{3,2},{4,5},{5,4},{6,7},{7,6},{8,9},{9,8},{10,11... | collective-permute-start | bytes 4177928 | tf_op jit(solution)/shard_map/ppermute | solution.py:28
  101.7 35.2 %copy-start.10 = (f32[512,1]{1,0:T(8,128)S(1)}, f32[512,1]{1,0:T(8,128)}, u32[]{:S(2)}) copy-start(f32[512,1]{1,0:T(8,128)} %copy-done.9) | copy-start | bytes 6148
  102.1 37.9 %copy-start.8 = (bf16[2,256,896]{2,1,0:T(8,128)(2,1)S(1)}, bf16[2,256,896]{2,1,0:T(8,128)(2,1)}, u32[]{:S(2)}) copy-start(bf16[2,256,896]{2,1,0:T(8,128)(2,1)} %copy-done.7) | copy-start | bytes 2752516
  102.1 5.6 %collective-permute-start.31 = (f32[1,1280]{1,0:T(1,128)S(1)}, f32[1,1280]{1,0:T(1,128)S(1)}, u32[]{:S(2)}, u32[]{:S(2)}) collective-permute-start(f32[1,1280]{1,0:T(1,128)S(1)} %slice_bitcast_fusion.5), channel_id=1, source_target_pairs={{0,32},{32,0},{64,96},{96,64},{128,160},{160,128},{192,224},{224,1... | collective-permute-start | bytes 15368 | tf_op jit(solution)/shard_map/ppermute | solution.py:28
  102.2 40.6 %copy-start.14 = (bf16[640]{0:T(1024)(128)(2,1)S(1)}, bf16[640]{0:T(1024)(128)(2,1)}, u32[]{:S(2)}) copy-start(bf16[640]{0:T(1024)(128)(2,1)} %param.5) | copy-start | bytes 3844
  103.2 35.5 %collective-permute-start.23 = (bf16[272,640]{1,0:T(8,128)(2,1)}, bf16[272,640]{1,0:T(8,128)(2,1)S(1)}, u32[]{:S(2)}, u32[]{:S(2)}) collective-permute-start(bf16[272,640]{1,0:T(8,128)(2,1)} %get-tuple-element.64), channel_id=1, source_target_pairs={{0,2},{2,0},{4,6},{6,4},{1,3},{3,1},{5,7},{7,5},{8,10},{10,8},{12,... | collective-permute-start | bytes 1044488 | tf_op jit(solution)/shard_map/ppermute | solution.py:28
  105.7 33.0 %collective-permute-start.25 = (bf16[272,640]{1,0:T(8,128)(2,1)}, bf16[272,640]{1,0:T(8,128)(2,1)}, u32[]{:S(2)}, u32[]{:S(2)}) collective-permute-start(bf16[272,640]{1,0:T(8,128)(2,1)} %get-tuple-element.65), channel_id=1, source_target_pairs={{0,6},{2,4},{4,2},{6,0},{1,7},{3,5},{5,3},{7,1},{8,14},{10,12},{12... | collective-permute-start | bytes 1044488 | tf_op jit(solution)/shard_map/ppermute | solution.py:28
  107.0 31.6 %collective-permute-start.24 = (bf16[272,640]{1,0:T(8,128)(2,1)S(1)}, bf16[272,640]{1,0:T(8,128)(2,1)}, u32[]{:S(2)}, u32[]{:S(2)}) collective-permute-start(bf16[272,640]{1,0:T(8,128)(2,1)S(1)} %get-tuple-element.66), channel_id=1, source_target_pairs={{0,4},{2,6},{4,0},{6,2},{1,5},{3,7},{5,1},{7,3},{8,12},{10,14},{12... | collective-permute-start | bytes 1044488 | tf_op jit(solution)/shard_map/ppermute | solution.py:28
  107.8 5.1 %collective-permute-start.32 = (f32[1,1280]{1,0:T(1,128)S(1)}, f32[1,1280]{1,0:T(1,128)S(1)}, u32[]{:S(2)}, u32[]{:S(2)}) collective-permute-start(f32[1,1280]{1,0:T(1,128)S(1)} %fusion.2), channel_id=1, source_target_pairs={{0,64},{32,96},{64,0},{96,32},{128,192},{160,224},{192,128},{224,1... | collective-permute-start | bytes 15368 | tf_op jit(solution)/shard_map/ppermute | solution.py:28
  112.9 7.9 %collective-permute-start.33 = (f32[1,1280]{1,0:T(1,128)S(1)}, f32[1,1280]{1,0:T(1,128)S(1)}, u32[]{:S(2)}, u32[]{:S(2)}) collective-permute-start(f32[1,1280]{1,0:T(1,128)S(1)} %add.165), channel_id=1, source_target_pairs={{0,128},{32,160},{64,192},{96,224},{128,0},{160,32},{192,64},{224,... | collective-permute-start | bytes 15368 | tf_op jit(solution)/shard_map/ppermute | solution.py:28
  120.8 3.7 %collective-permute-start.34 = (f32[1,1280]{1,0:T(1,128)S(1)}, f32[1,1280]{1,0:T(1,128)S(1)}, u32[]{:S(2)}, u32[]{:S(2)}) collective-permute-start(f32[1,1280]{1,0:T(1,128)S(1)} %add.166), channel_id=1, source_target_pairs={{0,8},{8,0},{16,24},{24,16},{1,9},{9,1},{17,25},{25,17},{2,10},{10... | collective-permute-start | bytes 15368 | tf_op jit(solution)/shard_map/ppermute | solution.py:28
  124.5 5.2 %collective-permute-start.35 = (f32[1,1280]{1,0:T(1,128)S(1)}, f32[1,1280]{1,0:T(1,128)S(1)}, u32[]{:S(2)}, u32[]{:S(2)}) collective-permute-start(f32[1,1280]{1,0:T(1,128)S(1)} %add.167), channel_id=1, source_target_pairs={{0,16},{8,24},{16,0},{24,8},{1,17},{9,25},{17,1},{25,9},{2,18},{10... | collective-permute-start | bytes 15368 | tf_op jit(solution)/shard_map/ppermute | solution.py:28
  129.7 5.2 %collective-permute-start.36 = (f32[1,1280]{1,0:T(1,128)S(1)}, f32[1,1280]{1,0:T(1,128)S(1)}, u32[]{:S(2)}, u32[]{:S(2)}) collective-permute-start(f32[1,1280]{1,0:T(1,128)S(1)} %add.168), channel_id=1, source_target_pairs={{0,4},{4,0},{1,5},{5,1},{2,6},{6,2},{3,7},{7,3},{8,12},{12,8},{9,1... | collective-permute-start | bytes 15368 | tf_op jit(solution)/shard_map/ppermute | solution.py:28
  135.0 3.7 %collective-permute-start.37 = (f32[1,640]{1,0:T(1,128)S(1)}, f32[1,640]{1,0:T(1,128)S(1)}, u32[]{:S(2)}, u32[]{:S(2)}) collective-permute-start(f32[1,640]{1,0:T(1,128)S(1)} %slice.62), channel_id=1, source_target_pairs={{0,2},{2,0},{1,3},{3,1},{4,6},{6,4},{5,7},{7,5},{8,10},{10,8},{9,1... | collective-permute-start | bytes 7688 | tf_op jit(solution)/shard_map/ppermute | solution.py:28
  140.0 14.8 %collective-permute-start.26 = (bf16[256,896]{1,0:T(8,128)(2,1)S(1)}, bf16[256,896]{1,0:T(8,128)(2,1)S(1)}, u32[]{:S(2)}, u32[]{:S(2)}) collective-permute-start(bf16[256,896]{1,0:T(8,128)(2,1)S(1)} %slice_bitcast_fusion), channel_id=1, source_target_pairs={{0,4},{4,0},{1,5},{5,1},{2,6},{6,2},{3,7},{7,3},{8,12},{12,8},{9,1... | collective-permute-start | bytes 1376264 | tf_op jit(solution)/shard_map/ppermute | solution.py:28
  150.5 5.6 %collective-permute-start.27 = (bf16[80,896]{1,0:T(8,128)(2,1)S(1)}, bf16[80,896]{1,0:T(8,128)(2,1)S(1)}, u32[]{:S(2)}, u32[]{:S(2)}) collective-permute-start(bf16[80,896]{1,0:T(8,128)(2,1)S(1)} %get-tuple-element.71), channel_id=1, source_target_pairs={{0,8},{8,0},{16,24},{24,16},{1,9},{9,1},{17,25},{25,17},{2,10},{10... | collective-permute-start | bytes 430088 | tf_op jit(solution)/shard_map/ppermute | solution.py:28
  152.0 9.6 %collective-permute-start.29 = (bf16[80,896]{1,0:T(8,128)(2,1)S(1)}, bf16[80,896]{1,0:T(8,128)(2,1)S(1)}, u32[]{:S(2)}, u32[]{:S(2)}) collective-permute-start(bf16[80,896]{1,0:T(8,128)(2,1)S(1)} %get-tuple-element.72), channel_id=1, source_target_pairs={{0,24},{8,16},{16,8},{24,0},{1,25},{9,17},{17,9},{25,1},{2,26},{10... | collective-permute-start | bytes 430088 | tf_op jit(solution)/shard_map/ppermute | solution.py:28
  154.1 7.5 %collective-permute-start.28 = (bf16[80,896]{1,0:T(8,128)(2,1)S(1)}, bf16[80,896]{1,0:T(8,128)(2,1)S(1)}, u32[]{:S(2)}, u32[]{:S(2)}) collective-permute-start(bf16[80,896]{1,0:T(8,128)(2,1)S(1)} %get-tuple-element.73), channel_id=1, source_target_pairs={{0,16},{8,24},{16,0},{24,8},{1,17},{9,25},{17,1},{25,9},{2,18},{10... | collective-permute-start | bytes 430088 | tf_op jit(solution)/shard_map/ppermute | solution.py:28
  162.6 5.9 %collective-permute-start.30 = (bf16[40,896]{1,0:T(8,128)(2,1)S(1)}, bf16[40,896]{1,0:T(8,128)(2,1)S(1)}, u32[]{:S(2)}, u32[]{:S(2)}) collective-permute-start(bf16[40,896]{1,0:T(8,128)(2,1)S(1)} %dynamic-slice_convert_fusion), channel_id=1, source_target_pairs={{0,4},{4,0},{1,5},{5,1},{2,6},{6,2},{3,7},{7,3},{8,12},{12,8},{9,1... | collective-permute-start | bytes 215048 | tf_op jit(solution)/shard_map/ppermute | solution.py:28
  (6 other events, 8.1 us)
Sparse Core Ops, SparseCore 0:
  91.4 57.9 reduce-scatter.1
where the time goes:
time: 176 us
  waiting for transfers between devices  66.5 us (38%)
  starting transfers between devices  60.2 us (34%)
  between operations  14.5 us (8%)
  Pallas kernels  12.6 us (7%)
  local copies, waits for them, and re-layouts  9.54 us (5%)
  other arithmetic  8.14 us (5%)
  matrix products  4.58 us (3%)
    ppermute x31, starting transfers between devices, flip(): return lax.ppermute(a, axis, [(i, i ^ bit) for i in range(n)])  52.7 us
    ppermute x31, waiting for transfers between devices, flip(): return lax.ppermute(a, axis, [(i, i ^ bit) for i in range(n)])  49.8 us
    ppermute x7, waiting for transfers between devices, ring(): return lax.ppermute(a, 'z', [(i, (i + d) % n) for i in range(n)])  11.5 us
    ppermute x7, starting transfers between devices, ring(): return lax.ppermute(a, 'z', [(i, (i + d) % n) for i in range(n)])  7.41 us
    pallas_call x2, Pallas kernels, back_call(): pl.pallas_call(back_kernel, out_shape=jax.ShapeDtypeStruct((groups, tok +...  6.02 us
    unnamed x30, local copies, waits for them, and re-layouts  5.9 us
    reduce_scatter x1, waiting for transfers between devices, body(): sums_z = lax.psum_scatter(terms, 'z', scatter_dimension=0, tiled=True)  5.16 us
    dot_general x1, matrix products, body(): lax.dot_general(normed, grad, TN, preferred_element_type=F32).astype(BF)  4.58 us
  transfers between devices with their start and end apart: 39, of which 22 were waited for; matrix products, arithmetic and copies ran while one was open for 4% of the time, Pallas kernels for 5%

commit v1 on v0

--- a/solution.py
+++ b/solution.py
@@ -205,7 +205,7 @@
     w_b = w_b + [flip(w_b[0], "y", k) for k in (1, 2, 3)]
     w_a = w[None, None, None, :, :PART_A]
     w_a = pair(z // 4, w_a, flip(w_a, "z", 4), 0)
-    *w_b, stream = together(*w_b, stream)
+    *w_b, stream, act_grad = together(*w_b, stream, act_grad)
     w_b = jnp.concatenate(ordered(w_b, y), axis=0)
     held = jnp.zeros((NUM["z"], *w_b.shape), BF)
     put = lambda held, block, i: lax.dynamic_update_index_in_dim(held, block, lax.rem(z + i, NUM["z"]), 0)
@@ -213,8 +213,6 @@
     up = down = w_b
     for step in (1, 2, 3):
         up, down = ring(up, 1), ring(down, -1)
-        if step == 1:
-            up, down, act_grad = together(up, down, act_grad)
         held = put(put(held, up, NUM["z"] - step), down, step)
         if step < 3:
             w_a = pair((z // (4 >> step)) % 2, w_a, flip(w_a, "z", 4 >> step), step)

time: 176 us -> 176 us (level)
  starting transfers between devices: 60.2 us -> 51.2 us
  waiting for transfers between devices: 66.5 us -> 75.5 us
    ppermute x31, starting transfers between devices: 52.7 us -> 44.1 us  [flip(): return lax.ppermute(a, axis, [(i, i ^ bit) for i in range(n)])]
    ppermute x31, waiting for transfers between devices: 49.8 us -> 57.6 us  [flip(): return lax.ppermute(a, axis, [(i, i ^ bit) for i in range(n)])]
  transfers between devices with their start and end apart: 39 -> 39, of which waited for: 22 -> 21; matrix products, arithmetic and copies ran while one was open for 4% -> 4% of each run, Pallas kernels for 5% -> 5%
where the time goes in v1:
time: 176 us
  waiting for transfers between devices  75.5 us (43%)
  starting transfers between devices  51.2 us (29%)
  between operations  14.6 us (8%)
  Pallas kernels  12.6 us (7%)
  local copies, waits for them, and re-layouts  9.53 us (5%)
  other arithmetic  8.14 us (5%)
  matrix products  4.58 us (3%)
    ppermute x31, waiting for transfers between devices, flip(): return lax.ppermute(a, axis, [(i, i ^ bit) for i in range(n)])  57.6 us
    ppermute x31, starting transfers between devices, flip(): return lax.ppermute(a, axis, [(i, i ^ bit) for i in range(n)])  44.1 us
    ppermute x7, waiting for transfers between devices, ring(): return lax.ppermute(a, 'z', [(i, (i + d) % n) for i in range(n)])  13 us
    ppermute x7, starting transfers between devices, ring(): return lax.ppermute(a, 'z', [(i, (i + d) % n) for i in range(n)])  7.04 us
    pallas_call x2, Pallas kernels, back_call(): pl.pallas_call(back_kernel, out_shape=jax.ShapeDtypeStruct((groups, tok +...  6.03 us
    unnamed x30, local copies, waits for them, and re-layouts  5.9 us
    reduce_scatter x1, waiting for transfers between devices, body(): sums_z = lax.psum_scatter(terms, 'z', scatter_dimension=0, tiled=True)  4.82 us
    dot_general x1, matrix products, body(): lax.dot_general(normed, grad, TN, preferred_element_type=F32).astype(BF)  4.58 us
  transfers between devices with their start and end apart: 39, of which 21 were waited for; matrix products, arithmetic and copies ran while one was open for 4% of the time, Pallas kernels for 5%

profile of v1, /device:TPU:2, one launch (start us, length us, event | category | flops | bytes accessed | tf_op | source)
XLA Modules:
  0.0 176.1 jit_solution(3255679049850075532)
XLA Ops:
  8.1 2.1 %collective-permute-start = (bf16[40,896]{1,0:T(8,128)(2,1)S(1)}, bf16[40,896]{1,0:T(8,128)(2,1)S(1)}, u32[]{:S(2)}, u32[]{:S(2)}) collective-permute-start(bf16[40,896]{1,0:T(8,128)(2,1)S(1)} %constant_dynamic-slice_fusion.4), channel_id=1, source_target_pairs={{0,4},{4,0},{1,5},{5,1},{2,6},{6,2},{3,7},{7,3},{8,12},{12,8},{9,1... | collective-permute-start | bytes 215048 | tf_op jit(solution)/shard_map/ppermute | solution.py:28
  10.3 3.6 %collective-permute-done = bf16[40,896]{1,0:T(8,128)(2,1)S(1)} collective-permute-done((bf16[40,896]{1,0:T(8,128)(2,1)S(1)}, bf16[40,896]{1,0:T(8,128)(2,1)S(1)}, u32[]{:S(2)}, u32[]{:S(2)}) %collective-permute-start) | collective-permute-done | bytes 71712 | tf_op jit(solution)/shard_map/ppermute | solution.py:28
  14.9 7.3 %collective-permute-start.1 = (bf16[1,1,1,80,384]{4,3,2,1,0:T(8,128)(2,1)S(1)}, bf16[1,1,1,80,384]{4,3,2,1,0:T(8,128)(2,1)S(1)}, u32[]{:S(2)}, u32[]{:S(2)}) collective-permute-start(bf16[1,1,1,80,384]{4,3,2,1,0:T(8,128)(2,1)S(1)} %maximum_bitcast_fusion), channel_id=1, source_target_pairs={{0,128},{32,160},{64,192},{96,224},{128,0},{160,32},{192,64},{224,... | collective-permute-start | bytes 184328 | tf_op jit(solution)/shard_map/ppermute | solution.py:28
  22.2 3.0 %collective-permute-start.9 = (bf16[80,512]{1,0:T(8,128)(2,1)S(1)}, bf16[80,512]{1,0:T(8,128)(2,1)S(1)}, u32[]{:S(2)}, u32[]{:S(2)}) collective-permute-start(bf16[80,512]{1,0:T(8,128)(2,1)S(1)} %pad_maximum_fusion.9), channel_id=1, source_target_pairs={{0,24},{8,16},{16,8},{24,0},{1,25},{9,17},{17,9},{25,1},{2,26},{10... | collective-permute-start | bytes 245768 | tf_op jit(solution)/shard_map/ppermute | solution.py:28
  26.3 1.6 collective-permute-start.2
  28.7 2.4 %collective-permute-done.8 = bf16[80,512]{1,0:T(8,128)(2,1)S(1)} collective-permute-done((bf16[80,512]{1,0:T(8,128)(2,1)S(1)}, bf16[80,512]{1,0:T(8,128)(2,1)S(1)}, u32[]{:S(2)}, u32[]{:S(2)}) %collective-permute-start.8) | collective-permute-done | bytes 81952 | tf_op jit(solution)/shard_map/ppermute | solution.py:28
  31.2 1.1 collective-permute-start.15
  32.3 2.2 %collective-permute-start.16 = (bf16[320,512]{1,0:T(8,128)(2,1)S(1)}, bf16[320,512]{1,0:T(8,128)(2,1)S(1)}, u32[]{:S(2)}, u32[]{:S(2)}) collective-permute-start(bf16[320,512]{1,0:T(8,128)(2,1)S(1)} %pad_maximum_fusion.6), channel_id=1, source_target_pairs={{0,224},{32,0},{64,32},{96,64},{128,96},{160,128},{192,160},{224,1... | collective-permute-start | bytes 983048 | tf_op jit(solution)/shard_map/ppermute | solution.py:37
  34.6 2.2 %collective-permute-start.11 = (bf16[272,640]{1,0:T(8,128)(2,1)S(1)}, bf16[272,640]{1,0:T(8,128)(2,1)S(1)}, u32[]{:S(2)}, u32[]{:S(2)}) collective-permute-start(bf16[272,640]{1,0:T(8,128)(2,1)S(1)} %get-tuple-element.75), channel_id=1, source_target_pairs={{0,4},{2,6},{4,0},{6,2},{1,5},{3,7},{5,1},{7,3},{8,12},{10,14},{12... | collective-permute-start | bytes 1044488 | tf_op jit(solution)/shard_map/ppermute | solution.py:28
  36.8 1.4 collective-permute-start.10
  39.6 2.1 %collective-permute-start.14 = (bf16[256,896]{1,0:T(8,128)(2,1)S(1)}, bf16[256,896]{1,0:T(8,128)(2,1)S(1)}, u32[]{:S(2)}, u32[]{:S(2)}) collective-permute-start(bf16[256,896]{1,0:T(8,128)(2,1)S(1)} %get-tuple-element.66), channel_id=1, source_target_pairs={{0,4},{4,0},{1,5},{5,1},{2,6},{6,2},{3,7},{7,3},{8,12},{12,8},{9,1... | collective-permute-start | bytes 1376264 | tf_op jit(solution)/shard_map/ppermute | solution.py:28
  42.1 5.3 %collective-permute-done.11 = bf16[272,640]{1,0:T(8,128)(2,1)S(1)} collective-permute-done((bf16[272,640]{1,0:T(8,128)(2,1)S(1)}, bf16[272,640]{1,0:T(8,128)(2,1)S(1)}, u32[]{:S(2)}, u32[]{:S(2)}) %collective-permute-start.11) | collective-permute-done | bytes 348192 | tf_op jit(solution)/shard_map/ppermute | solution.py:28
  47.4 7.4 %collective-permute-done.10 = bf16[272,640]{1,0:T(8,128)(2,1)S(1)} collective-permute-done((bf16[272,640]{1,0:T(8,128)(2,1)S(1)}, bf16[272,640]{1,0:T(8,128)(2,1)S(1)}, u32[]{:S(2)}, u32[]{:S(2)}) %collective-permute-start.10) | collective-permute-done | bytes 348192 | tf_op jit(solution)/shard_map/ppermute | solution.py:28
  55.3 1.5 collective-permute-start.6
  56.8 3.3 %collective-permute-done.14 = bf16[256,896]{1,0:T(8,128)(2,1)S(1)} collective-permute-done((bf16[256,896]{1,0:T(8,128)(2,1)S(1)}, bf16[256,896]{1,0:T(8,128)(2,1)S(1)}, u32[]{:S(2)}, u32[]{:S(2)}) %collective-permute-start.14) | collective-permute-done | bytes 458784 | tf_op jit(solution)/shard_map/ppermute | solution.py:28
  60.2 1.7 collective-permute-start.5
  62.1 3.2 %collective-permute-start.20 = (bf16[320,512]{1,0:T(8,128)(2,1)S(1)}, bf16[320,512]{1,0:T(8,128)(2,1)S(1)}, u32[]{:S(2)}, u32[]{:S(2)}) collective-permute-start(bf16[320,512]{1,0:T(8,128)(2,1)S(1)} %collective-permute-done.18), channel_id=1, source_target_pairs={{0,224},{32,0},{64,32},{96,64},{128,96},{160,128},{192,160},{224,1... | collective-permute-start | bytes 983048 | tf_op jit(solution)/shard_map/ppermute | solution.py:37
  65.4 5.0 %collective-permute-done.19 = bf16[320,512]{1,0:T(8,128)(2,1)S(1)} collective-permute-done((bf16[320,512]{1,0:T(8,128)(2,1)S(1)}, bf16[320,512]{1,0:T(8,128)(2,1)S(1)}, u32[]{:S(2)}, u32[]{:S(2)}) %collective-permute-start.19) | collective-permute-done | bytes 327712 | tf_op jit(solution)/shard_map/ppermute | solution.py:37
  71.3 7.8 %collective-permute-done.21 = bf16[320,512]{1,0:T(8,128)(2,1)S(1)} collective-permute-done((bf16[320,512]{1,0:T(8,128)(2,1)S(1)}, bf16[320,512]{1,0:T(8,128)(2,1)S(1)}, u32[]{:S(2)}, u32[]{:S(2)}) %collective-permute-start.21) | collective-permute-done | bytes 327712 | tf_op jit(solution)/shard_map/ppermute | solution.py:37
  79.2 2.1 %norm.1 = (bf16[512,2560]{1,0:T(8,128)(2,1)S(1)}, f32[512,1]{1,0:T(8,128)S(1)}, f32[1,2560]{1,0:T(1,128)S(1)}) custom-call(s32[2]{0:T(128)S(1)} %pad_add_fusion.place, bf16[2,2,272,640]{3,2,1,0:T(8,128)(2,1)S(1)} %bitcast.75, bf16[2,2,272,640]{3,2,1,0:T(8,128)(2,1)S(1)} %collective-permute-done.13.other), custom_call_target="tpu_custom_call" | custom-call | flops 5242880 | bytes 5242880 | tf_op jit(solution)/shard_map/norm/pallas_call | solution.py:79
  82.0 2.2 %gate.2 = (bf16[2,256,384]{2,1,0:T(8,128)(2,1)S(1)}, bf16[512,384]{1,0:T(8,128)(2,1)S(1)}, f32[512,1]{1,0:T(8,128)S(1)}) custom-call(bf16[512,2560]{1,0:T(8,128)(2,1)S(1)} %get-tuple-element.32.refs_0_.normed, bf16[2560,384]{1,0:T(8,128)(2,1)S(1)} %bitcast.71, bf16[2,256,896]{2,1,0:T(8,128)(2,1)S(1)} %pad_maximum_fusion.2.refs_2_), custom_call_target="tpu_custom_call" | custom-call | flops 1006632960 | bytes 4587520 | tf_op jit(solution)/shard_map/gate/pallas_call | solution.py:126
  84.2 2.3 %gate.3 = (bf16[2,256,896]{2,1,0:T(8,128)(2,1)S(1)}, bf16[512,896]{1,0:T(8,128)(2,1)S(1)}, f32[512,1]{1,0:T(8,128)S(1)}) custom-call(bf16[512,2560]{1,0:T(8,128)(2,1)S(1)} %get-tuple-element.32.refs_0_.normed, bf16[2560,512]{1,0:T(8,128)(2,1)S(1)} %bitcast.68, bf16[2,256,896]{2,1,0:T(8,128)(2,1)S(1)} %pad_maximum_fusion.2.refs_2_, ...), custom_call_target="tpu_custom_call" | custom-call | flops 1342177280 | bytes 5242880 | tf_op jit(solution)/shard_map/gate/pallas_call | solution.py:126
  88.2 4.6 %convolution_convert_fusion = bf16[2560,896]{1,0:T(8,128)(2,1)} fusion(bf16[512,2560]{1,0:T(8,128)(2,1)S(1)} %get-tuple-element.32.refs_0_.normed, bf16[512,896]{1,0:T(8,128)(2,1)S(1)} %get-tuple-element.47.grad), kind=kOutput, calls=%fused_computation | convolution fusion | flops 2351104000 | bytes 8126464 | tf_op jit(solution)/shard_map/dot_general | solution.py:235
  92.8 1.7 copy-done.1
  94.5 1.5 copy-done.3
  97.0 3.0 %back.3 = bf16[2,272,1280]{2,1,0:T(8,128)(2,1)S(1)} custom-call(s32[2]{0:T(128)S(1)} %pad_add_fusion.place, bf16[512,896]{1,0:T(8,128)(2,1)S(1)} %get-tuple-element.47.grad, bf16[2560,384]{1,0:T(8,128)(2,1)S(1)} %bitcast.72, bf16[2560,512]{1,0:T(8,128)(2,1)S(1)} %bitcast.69, bf16[512,2560]{1,0:T(8,128)(2,1)S(1)} %get-tuple-element.32.refs_0_.normed, ...), custom_call_target="tpu_custom_call" | custom-call | flops 1174405120 | bytes 6225920 | tf_op jit(solution)/shard_map/back/pallas_call | solution.py:170
  100.2 3.0 %back.2 = bf16[2,272,1280]{2,1,0:T(8,128)(2,1)S(1)} custom-call(s32[2]{0:T(128)S(1)} %pad_add_fusion.place, bf16[512,896]{1,0:T(8,128)(2,1)S(1)} %get-tuple-element.47.grad, bf16[2560,384]{1,0:T(8,128)(2,1)S(1)} %bitcast.73, bf16[2560,512]{1,0:T(8,128)(2,1)S(1)} %bitcast.70, bf16[512,2560]{1,0:T(8,128)(2,1)S(1)} %get-tuple-element.32.refs_0_.normed, ...), custom_call_target="tpu_custom_call" | custom-call | flops 1174405120 | bytes 6225920 | tf_op jit(solution)/shard_map/back/pallas_call | solution.py:170
  103.7 2.1 %collective-permute-start.31 = (f32[1,1280]{1,0:T(1,128)S(1)}, f32[1,1280]{1,0:T(1,128)S(1)}, u32[]{:S(2)}, u32[]{:S(2)}) collective-permute-start(f32[1,1280]{1,0:T(1,128)S(1)} %slice_bitcast_fusion.5), channel_id=1, source_target_pairs={{0,32},{32,0},{64,96},{96,64},{128,160},{160,128},{192,224},{224,1... | collective-permute-start | bytes 15368 | tf_op jit(solution)/shard_map/ppermute | solution.py:28
  107.3 3.5 %collective-permute-start.24 = (bf16[272,640]{1,0:T(8,128)(2,1)S(1)}, bf16[272,640]{1,0:T(8,128)(2,1)}, u32[]{:S(2)}, u32[]{:S(2)}) collective-permute-start(bf16[272,640]{1,0:T(8,128)(2,1)S(1)} %get-tuple-element.62), channel_id=1, source_target_pairs={{0,4},{2,6},{4,0},{6,2},{1,5},{3,7},{5,1},{7,3},{8,12},{10,14},{12... | collective-permute-start | bytes 1044488 | tf_op jit(solution)/shard_map/ppermute | solution.py:28
  111.2 4.5 %collective-permute-done.32 = f32[1,1280]{1,0:T(1,128)S(1)} collective-permute-done((f32[1,1280]{1,0:T(1,128)S(1)}, f32[1,1280]{1,0:T(1,128)S(1)}, u32[]{:S(2)}, u32[]{:S(2)}) %collective-permute-start.32) | collective-permute-done | bytes 5152 | tf_op jit(solution)/shard_map/ppermute | solution.py:28
  115.7 1.5 collective-permute-start.33
  117.2 6.4 %collective-permute-done.33 = f32[1,1280]{1,0:T(1,128)S(1)} collective-permute-done((f32[1,1280]{1,0:T(1,128)S(1)}, f32[1,1280]{1,0:T(1,128)S(1)}, u32[]{:S(2)}, u32[]{:S(2)}) %collective-permute-start.33) | collective-permute-done | bytes 5152 | tf_op jit(solution)/shard_map/ppermute | solution.py:28
  124.2 3.1 %collective-permute-done.34 = f32[1,1280]{1,0:T(1,128)S(1)} collective-permute-done((f32[1,1280]{1,0:T(1,128)S(1)}, f32[1,1280]{1,0:T(1,128)S(1)}, u32[]{:S(2)}, u32[]{:S(2)}) %collective-permute-start.34) | collective-permute-done | bytes 5152 | tf_op jit(solution)/shard_map/ppermute | solution.py:28
  127.3 2.1 %collective-permute-start.35 = (f32[1,1280]{1,0:T(1,128)S(1)}, f32[1,1280]{1,0:T(1,128)S(1)}, u32[]{:S(2)}, u32[]{:S(2)}) collective-permute-start(f32[1,1280]{1,0:T(1,128)S(1)} %add.167), channel_id=1, source_target_pairs={{0,16},{8,24},{16,0},{24,8},{1,17},{9,25},{17,1},{25,9},{2,18},{10... | collective-permute-start | bytes 15368 | tf_op jit(solution)/shard_map/ppermute | solution.py:28
  129.4 3.1 %collective-permute-done.35 = f32[1,1280]{1,0:T(1,128)S(1)} collective-permute-done((f32[1,1280]{1,0:T(1,128)S(1)}, f32[1,1280]{1,0:T(1,128)S(1)}, u32[]{:S(2)}, u32[]{:S(2)}) %collective-permute-start.35) | collective-permute-done | bytes 5152 | tf_op jit(solution)/shard_map/ppermute | solution.py:28
  132.8 4.9 %collective-permute-done.36 = f32[1,1280]{1,0:T(1,128)S(1)} collective-permute-done((f32[1,1280]{1,0:T(1,128)S(1)}, f32[1,1280]{1,0:T(1,128)S(1)}, u32[]{:S(2)}, u32[]{:S(2)}) %collective-permute-start.36) | collective-permute-done | bytes 5152 | tf_op jit(solution)/shard_map/ppermute | solution.py:28
  138.5 3.0 %collective-permute-done.37 = f32[1,640]{1,0:T(1,128)S(1)} collective-permute-done((f32[1,640]{1,0:T(1,128)S(1)}, f32[1,640]{1,0:T(1,128)S(1)}, u32[]{:S(2)}, u32[]{:S(2)}) %collective-permute-start.37) | collective-permute-done | bytes 2592 | tf_op jit(solution)/shard_map/ppermute | solution.py:28
  141.5 1.3 fusion
  144.6 4.8 %reduce-scatter.2.cloned.1.call-done = bf16[320,896]{1,0:T(8,128)(2,1)} async-done(((bf16[2560,896]{1,0:T(8,128)(2,1)}), bf16[320,896]{1,0:T(8,128)(2,1)}) %reduce-scatter.2.cloned.1.call-update) | async-done | bytes 573456 | tf_op jit(solution)/shard_map/reduce_scatter | solution.py:237
  149.4 1.1 constant_dynamic-slice_fusion.2
  150.5 1.6 collective-permute-start.27
  152.0 2.1 %collective-permute-start.29 = (bf16[80,896]{1,0:T(8,128)(2,1)S(1)}, bf16[80,896]{1,0:T(8,128)(2,1)S(1)}, u32[]{:S(2)}, u32[]{:S(2)}) collective-permute-start(bf16[80,896]{1,0:T(8,128)(2,1)S(1)} %get-tuple-element.68), channel_id=1, source_target_pairs={{0,24},{8,16},{16,8},{24,0},{1,25},{9,17},{17,9},{25,1},{2,26},{10... | collective-permute-start | bytes 430088 | tf_op jit(solution)/shard_map/ppermute | solution.py:28
  154.8 1.2 collective-permute-done.27
  156.1 5.5 %collective-permute-done.29 = bf16[80,896]{1,0:T(8,128)(2,1)S(1)} collective-permute-done((bf16[80,896]{1,0:T(8,128)(2,1)S(1)}, bf16[80,896]{1,0:T(8,128)(2,1)S(1)}, u32[]{:S(2)}, u32[]{:S(2)}) %collective-permute-start.29) | collective-permute-done | bytes 143392 | tf_op jit(solution)/shard_map/ppermute | solution.py:28
  161.6 1.0 convert_add_fusion.2
  162.6 2.2 %collective-permute-start.30 = (bf16[40,896]{1,0:T(8,128)(2,1)S(1)}, bf16[40,896]{1,0:T(8,128)(2,1)S(1)}, u32[]{:S(2)}, u32[]{:S(2)}) collective-permute-start(bf16[40,896]{1,0:T(8,128)(2,1)S(1)} %dynamic-slice_convert_fusion), channel_id=1, source_target_pairs={{0,4},{4,0},{1,5},{5,1},{2,6},{6,2},{3,7},{7,3},{8,12},{12,8},{9,1... | collective-permute-start | bytes 215048 | tf_op jit(solution)/shard_map/ppermute | solution.py:28
  164.8 1.0 pad_maximum_fusion.3
  165.7 2.8 %collective-permute-done.30 = bf16[40,896]{1,0:T(8,128)(2,1)S(1)} collective-permute-done((bf16[40,896]{1,0:T(8,128)(2,1)S(1)}, bf16[40,896]{1,0:T(8,128)(2,1)S(1)}, u32[]{:S(2)}, u32[]{:S(2)}) %collective-permute-start.30) | collective-permute-done | bytes 71712 | tf_op jit(solution)/shard_map/ppermute | solution.py:28
  (119 shorter events, 18.1 us)
Async XLA Ops:
  7.2 27.4 %copy-start.12 = (bf16[256,640]{1,0:T(8,128)(2,1)S(1)}, bf16[256,640]{1,0:T(8,128)(2,1)}, u32[]{:S(2)}) copy-start(bf16[256,640]{1,0:T(8,128)(2,1)} %param.4) | copy-start | bytes 983044
  7.2 27.4 %copy-start.13 = (bf16[640]{0:T(1024)(128)(2,1)S(1)}, bf16[640]{0:T(1024)(128)(2,1)}, u32[]{:S(2)}) copy-start(bf16[640]{0:T(1024)(128)(2,1)} %param.5) | copy-start | bytes 3844
  7.2 142.2 %reduce-scatter.2.cloned.1.call-start = ((), (), s32[]{:S(2)}) async-start(), calls=%async_computation.1 | async-start | bytes 5160960 | tf_op jit(solution)/shard_map/reduce_scatter | solution.py:237
  8.1 5.8 %collective-permute-start = (bf16[40,896]{1,0:T(8,128)(2,1)S(1)}, bf16[40,896]{1,0:T(8,128)(2,1)S(1)}, u32[]{:S(2)}, u32[]{:S(2)}) collective-permute-start(bf16[40,896]{1,0:T(8,128)(2,1)S(1)} %constant_dynamic-slice_fusion.4), channel_id=1, source_target_pairs={{0,4},{4,0},{1,5},{5,1},{2,6},{6,2},{3,7},{7,3},{8,12},{12,8},{9,1... | collective-permute-start | bytes 215048 | tf_op jit(solution)/shard_map/ppermute | solution.py:28
  14.9 11.4 %collective-permute-start.1 = (bf16[1,1,1,80,384]{4,3,2,1,0:T(8,128)(2,1)S(1)}, bf16[1,1,1,80,384]{4,3,2,1,0:T(8,128)(2,1)S(1)}, u32[]{:S(2)}, u32[]{:S(2)}) collective-permute-start(bf16[1,1,1,80,384]{4,3,2,1,0:T(8,128)(2,1)S(1)} %maximum_bitcast_fusion), channel_id=1, source_target_pairs={{0,128},{32,160},{64,192},{96,224},{128,0},{160,32},{192,64},{224,... | collective-permute-start | bytes 184328 | tf_op jit(solution)/shard_map/ppermute | solution.py:28
  22.2 6.5 %collective-permute-start.9 = (bf16[80,512]{1,0:T(8,128)(2,1)S(1)}, bf16[80,512]{1,0:T(8,128)(2,1)S(1)}, u32[]{:S(2)}, u32[]{:S(2)}) collective-permute-start(bf16[80,512]{1,0:T(8,128)(2,1)S(1)} %pad_maximum_fusion.9), channel_id=1, source_target_pairs={{0,24},{8,16},{16,8},{24,0},{1,25},{9,17},{17,9},{25,1},{2,26},{10... | collective-permute-start | bytes 245768 | tf_op jit(solution)/shard_map/ppermute | solution.py:28
  25.2 5.9 %collective-permute-start.8 = (bf16[80,512]{1,0:T(8,128)(2,1)S(1)}, bf16[80,512]{1,0:T(8,128)(2,1)S(1)}, u32[]{:S(2)}, u32[]{:S(2)}) collective-permute-start(bf16[80,512]{1,0:T(8,128)(2,1)S(1)} %pad_maximum_fusion.9), channel_id=1, source_target_pairs={{0,16},{8,24},{16,0},{24,8},{1,17},{9,25},{17,1},{25,9},{2,18},{10... | collective-permute-start | bytes 245768 | tf_op jit(solution)/shard_map/ppermute | solution.py:28
  25.8 5.3 %collective-permute-start.7 = (bf16[80,512]{1,0:T(8,128)(2,1)S(1)}, bf16[80,512]{1,0:T(8,128)(2,1)S(1)}, u32[]{:S(2)}, u32[]{:S(2)}) collective-permute-start(bf16[80,512]{1,0:T(8,128)(2,1)S(1)} %pad_maximum_fusion.9), channel_id=1, source_target_pairs={{0,8},{8,0},{16,24},{24,16},{1,9},{9,1},{17,25},{25,17},{2,10},{10... | collective-permute-start | bytes 245768 | tf_op jit(solution)/shard_map/ppermute | solution.py:28
  26.3 12.4 %collective-permute-start.2 = (bf16[2,1,1,80,384]{4,3,2,1,0:T(8,128)(2,1)S(1)}, bf16[2,1,1,80,384]{4,3,2,1,0:T(8,128)(2,1)S(1)}, u32[]{:S(2)}, u32[]{:S(2)}) collective-permute-start(bf16[2,1,1,80,384]{4,3,2,1,0:T(8,128)(2,1)S(1)} %pad_maximum_fusion.8), channel_id=1, source_target_pairs={{0,64},{32,96},{64,0},{96,32},{128,192},{160,224},{192,128},{224,1... | collective-permute-start | bytes 368648 | tf_op jit(solution)/shard_map/ppermute | solution.py:28
  31.2 7.3 %copy-start.11 = (bf16[256,1792]{1,0:T(8,128)(2,1)S(1)}, bf16[256,1792]{1,0:T(8,128)(2,1)}, u32[]{:S(2)}) copy-start(bf16[256,1792]{1,0:T(8,128)(2,1)} %param.7) | copy-start | bytes 2752516
  31.2 8.4 %collective-permute-start.15 = (bf16[320,512]{1,0:T(8,128)(2,1)S(1)}, bf16[320,512]{1,0:T(8,128)(2,1)S(1)}, u32[]{:S(2)}, u32[]{:S(2)}) collective-permute-start(bf16[320,512]{1,0:T(8,128)(2,1)S(1)} %pad_maximum_fusion.6), channel_id=1, source_target_pairs={{0,32},{32,64},{64,96},{96,128},{128,160},{160,192},{192,224},{224... | collective-permute-start | bytes 983048 | tf_op jit(solution)/shard_map/ppermute | solution.py:37
  32.3 9.4 %collective-permute-start.16 = (bf16[320,512]{1,0:T(8,128)(2,1)S(1)}, bf16[320,512]{1,0:T(8,128)(2,1)S(1)}, u32[]{:S(2)}, u32[]{:S(2)}) collective-permute-start(bf16[320,512]{1,0:T(8,128)(2,1)S(1)} %pad_maximum_fusion.6), channel_id=1, source_target_pairs={{0,224},{32,0},{64,32},{96,64},{128,96},{160,128},{192,160},{224,1... | collective-permute-start | bytes 983048 | tf_op jit(solution)/shard_map/ppermute | solution.py:37
  34.6 12.8 %collective-permute-start.11 = (bf16[272,640]{1,0:T(8,128)(2,1)S(1)}, bf16[272,640]{1,0:T(8,128)(2,1)S(1)}, u32[]{:S(2)}, u32[]{:S(2)}) collective-permute-start(bf16[272,640]{1,0:T(8,128)(2,1)S(1)} %get-tuple-element.75), channel_id=1, source_target_pairs={{0,4},{2,6},{4,0},{6,2},{1,5},{3,7},{5,1},{7,3},{8,12},{10,14},{12... | collective-permute-start | bytes 1044488 | tf_op jit(solution)/shard_map/ppermute | solution.py:28
  36.8 18.0 %collective-permute-start.10 = (bf16[272,640]{1,0:T(8,128)(2,1)S(1)}, bf16[272,640]{1,0:T(8,128)(2,1)S(1)}, u32[]{:S(2)}, u32[]{:S(2)}) collective-permute-start(bf16[272,640]{1,0:T(8,128)(2,1)S(1)} %get-tuple-element.75), channel_id=1, source_target_pairs={{0,2},{2,0},{4,6},{6,4},{1,3},{3,1},{5,7},{7,5},{8,10},{10,8},{12,... | collective-permute-start | bytes 1044488 | tf_op jit(solution)/shard_map/ppermute | solution.py:28
  38.7 16.2 %collective-permute-start.12 = (bf16[272,640]{1,0:T(8,128)(2,1)S(1)}, bf16[272,640]{1,0:T(8,128)(2,1)S(1)}, u32[]{:S(2)}, u32[]{:S(2)}) collective-permute-start(bf16[272,640]{1,0:T(8,128)(2,1)S(1)} %get-tuple-element.75), channel_id=1, source_target_pairs={{0,6},{2,4},{4,2},{6,0},{1,7},{3,5},{5,3},{7,1},{8,14},{10,12},{12... | collective-permute-start | bytes 1044488 | tf_op jit(solution)/shard_map/ppermute | solution.py:28
  39.6 20.6 %collective-permute-start.14 = (bf16[256,896]{1,0:T(8,128)(2,1)S(1)}, bf16[256,896]{1,0:T(8,128)(2,1)S(1)}, u32[]{:S(2)}, u32[]{:S(2)}) collective-permute-start(bf16[256,896]{1,0:T(8,128)(2,1)S(1)} %get-tuple-element.66), channel_id=1, source_target_pairs={{0,4},{4,0},{1,5},{5,1},{2,6},{6,2},{3,7},{7,3},{8,12},{12,8},{9,1... | collective-permute-start | bytes 1376264 | tf_op jit(solution)/shard_map/ppermute | solution.py:28
  41.8 13.4 %collective-permute-start.3 = (bf16[2,2,1,80,384]{4,3,2,1,0:T(8,128)(2,1)S(1)}, bf16[2,2,1,80,384]{4,3,2,1,0:T(8,128)(2,1)S(1)}, u32[]{:S(2)}, u32[]{:S(2)}) collective-permute-start(bf16[2,2,1,80,384]{4,3,2,1,0:T(8,128)(2,1)S(1)} %pad_maximum_fusion.7), channel_id=1, source_target_pairs={{0,32},{32,0},{64,96},{96,64},{128,160},{160,128},{192,224},{224,1... | collective-permute-start | bytes 737288 | tf_op jit(solution)/shard_map/ppermute | solution.py:28
  47.4 14.6 %collective-permute-start.17 = (bf16[320,512]{1,0:T(8,128)(2,1)S(1)}, bf16[320,512]{1,0:T(8,128)(2,1)S(1)}, u32[]{:S(2)}, u32[]{:S(2)}) collective-permute-start(bf16[320,512]{1,0:T(8,128)(2,1)S(1)} %collective-permute-done.15), channel_id=1, source_target_pairs={{0,32},{32,64},{64,96},{96,128},{128,160},{160,192},{192,224},{224... | collective-permute-start | bytes 983048 | tf_op jit(solution)/shard_map/ppermute | solution.py:37
  54.8 7.2 %collective-permute-start.18 = (bf16[320,512]{1,0:T(8,128)(2,1)S(1)}, bf16[320,512]{1,0:T(8,128)(2,1)S(1)}, u32[]{:S(2)}, u32[]{:S(2)}) collective-permute-start(bf16[320,512]{1,0:T(8,128)(2,1)S(1)} %collective-permute-done.16), channel_id=1, source_target_pairs={{0,224},{32,0},{64,32},{96,64},{128,96},{160,128},{192,160},{224,1... | collective-permute-start | bytes 983048 | tf_op jit(solution)/shard_map/ppermute | solution.py:37
  55.1 24.1 %collective-permute-start.13 = (bf16[2,2,272,640]{3,2,1,0:T(8,128)(2,1)S(1)}, bf16[2,2,272,640]{3,2,1,0:T(8,128)(2,1)S(1)}, u32[]{:S(2)}, u32[]{:S(2)}) collective-permute-start(bf16[2,2,272,640]{3,2,1,0:T(8,128)(2,1)S(1)} %bitcast.74), channel_id=1, source_target_pairs={{0,1},{1,0},{2,3},{3,2},{4,5},{5,4},{6,7},{7,6},{8,9},{9,8},{10,11... | collective-permute-start | bytes 4177928 | tf_op jit(solution)/shard_map/ppermute | solution.py:28
  55.3 25.9 %collective-permute-start.6 = (bf16[8,80,384]{2,1,0:T(8,128)(2,1)S(1)}, bf16[8,80,384]{2,1,0:T(8,128)(2,1)S(1)}, u32[]{:S(2)}, u32[]{:S(2)}) collective-permute-start(bf16[8,80,384]{2,1,0:T(8,128)(2,1)S(1)} %bitcast.76), channel_id=1, source_target_pairs={{0,24},{8,16},{16,8},{24,0},{1,25},{9,17},{17,9},{25,1},{2,26},{10... | collective-permute-start | bytes 1474568 | tf_op jit(solution)/shard_map/ppermute | solution.py:28
  60.2 21.1 %collective-permute-start.5 = (bf16[8,80,384]{2,1,0:T(8,128)(2,1)S(1)}, bf16[8,80,384]{2,1,0:T(8,128)(2,1)S(1)}, u32[]{:S(2)}, u32[]{:S(2)}) collective-permute-start(bf16[8,80,384]{2,1,0:T(8,128)(2,1)S(1)} %bitcast.77), channel_id=1, source_target_pairs={{0,16},{8,24},{16,0},{24,8},{1,17},{9,25},{17,1},{25,9},{2,18},{10... | collective-permute-start | bytes 1474568 | tf_op jit(solution)/shard_map/ppermute | solution.py:28
  62.0 8.4 %collective-permute-start.19 = (bf16[320,512]{1,0:T(8,128)(2,1)S(1)}, bf16[320,512]{1,0:T(8,128)(2,1)S(1)}, u32[]{:S(2)}, u32[]{:S(2)}) collective-permute-start(bf16[320,512]{1,0:T(8,128)(2,1)S(1)} %collective-permute-done.17), channel_id=1, source_target_pairs={{0,32},{32,64},{64,96},{96,128},{128,160},{160,192},{192,224},{224... | collective-permute-start | bytes 983048 | tf_op jit(solution)/shard_map/ppermute | solution.py:37
  62.1 8.7 %collective-permute-start.20 = (bf16[320,512]{1,0:T(8,128)(2,1)S(1)}, bf16[320,512]{1,0:T(8,128)(2,1)S(1)}, u32[]{:S(2)}, u32[]{:S(2)}) collective-permute-start(bf16[320,512]{1,0:T(8,128)(2,1)S(1)} %collective-permute-done.18), channel_id=1, source_target_pairs={{0,224},{32,0},{64,32},{96,64},{128,96},{160,128},{192,160},{224,1... | collective-permute-start | bytes 983048 | tf_op jit(solution)/shard_map/ppermute | solution.py:37
  70.3 11.0 %collective-permute-start.4 = (bf16[8,80,384]{2,1,0:T(8,128)(2,1)S(1)}, bf16[8,80,384]{2,1,0:T(8,128)(2,1)S(1)}, u32[]{:S(2)}, u32[]{:S(2)}) collective-permute-start(bf16[8,80,384]{2,1,0:T(8,128)(2,1)S(1)} %bitcast.78), channel_id=1, source_target_pairs={{0,8},{8,0},{16,24},{24,16},{1,9},{9,1},{17,25},{25,17},{2,10},{10... | collective-permute-start | bytes 1474568 | tf_op jit(solution)/shard_map/ppermute | solution.py:28
  70.8 8.3 %collective-permute-start.21 = (bf16[320,512]{1,0:T(8,128)(2,1)S(1)}, bf16[320,512]{1,0:T(8,128)(2,1)S(1)}, u32[]{:S(2)}, u32[]{:S(2)}) collective-permute-start(bf16[320,512]{1,0:T(8,128)(2,1)S(1)} %collective-permute-done.19), channel_id=1, source_target_pairs={{0,32},{32,64},{64,96},{96,128},{128,160},{160,192},{192,224},{224... | collective-permute-start | bytes 983048 | tf_op jit(solution)/shard_map/ppermute | solution.py:37
  79.1 5.1 %copy-start = (bf16[8,320,512]{2,1,0:T(8,128)(2,1)}, bf16[8,320,512]{2,1,0:T(8,128)(2,1)S(1)}, u32[]{:S(2)}) copy-start(bf16[8,320,512]{2,1,0:T(8,128)(2,1)S(1)} %bitcast_dynamic-update-slice_fusion) | copy-start | bytes 7864324
  82.0 2.2 %copy-start.2 = (bf16[8,4,80,384]{3,2,1,0:T(8,128)(2,1)}, bf16[8,4,80,384]{3,2,1,0:T(8,128)(2,1)S(1)}, u32[]{:S(2)}) copy-start(bf16[8,4,80,384]{3,2,1,0:T(8,128)(2,1)S(1)} %pad_maximum_fusion) | copy-start | bytes 5898244
  97.0 3.1 %copy-start.6 = (f32[512,1]{1,0:T(8,128)S(1)}, f32[512,1]{1,0:T(8,128)}, u32[]{:S(2)}) copy-start(f32[512,1]{1,0:T(8,128)} %copy-done.4) | copy-start | bytes 6148
  100.1 3.2 %collective-permute-start.22 = (bf16[2,272,1280]{2,1,0:T(8,128)(2,1)S(1)}, bf16[2,272,1280]{2,1,0:T(8,128)(2,1)S(1)}, u32[]{:S(2)}, u32[]{:S(2)}) collective-permute-start(bf16[2,272,1280]{2,1,0:T(8,128)(2,1)S(1)} %back.3), channel_id=1, source_target_pairs={{0,1},{1,0},{2,3},{3,2},{4,5},{5,4},{6,7},{7,6},{8,9},{9,8},{10,11... | collective-permute-start | bytes 4177928 | tf_op jit(solution)/shard_map/ppermute | solution.py:28
  103.2 35.2 %copy-start.10 = (f32[512,1]{1,0:T(8,128)S(1)}, f32[512,1]{1,0:T(8,128)}, u32[]{:S(2)}) copy-start(f32[512,1]{1,0:T(8,128)} %copy-done.9) | copy-start | bytes 6148
  103.6 39.2 %copy-start.8 = (bf16[2,256,896]{2,1,0:T(8,128)(2,1)S(1)}, bf16[2,256,896]{2,1,0:T(8,128)(2,1)}, u32[]{:S(2)}) copy-start(bf16[2,256,896]{2,1,0:T(8,128)(2,1)} %copy-done.7) | copy-start | bytes 2752516
  103.7 7.2 %collective-permute-start.31 = (f32[1,1280]{1,0:T(1,128)S(1)}, f32[1,1280]{1,0:T(1,128)S(1)}, u32[]{:S(2)}, u32[]{:S(2)}) collective-permute-start(f32[1,1280]{1,0:T(1,128)S(1)} %slice_bitcast_fusion.5), channel_id=1, source_target_pairs={{0,32},{32,0},{64,96},{96,64},{128,160},{160,128},{192,224},{224,1... | collective-permute-start | bytes 15368 | tf_op jit(solution)/shard_map/ppermute | solution.py:28
  105.8 37.4 %copy-start.14 = (bf16[640]{0:T(1024)(128)(2,1)S(1)}, bf16[640]{0:T(1024)(128)(2,1)}, u32[]{:S(2)}) copy-start(bf16[640]{0:T(1024)(128)(2,1)} %param.5) | copy-start | bytes 3844
  106.7 34.8 %collective-permute-start.23 = (bf16[272,640]{1,0:T(8,128)(2,1)}, bf16[272,640]{1,0:T(8,128)(2,1)S(1)}, u32[]{:S(2)}, u32[]{:S(2)}) collective-permute-start(bf16[272,640]{1,0:T(8,128)(2,1)} %get-tuple-element.60), channel_id=1, source_target_pairs={{0,2},{2,0},{4,6},{6,4},{1,3},{3,1},{5,7},{7,5},{8,10},{10,8},{12,... | collective-permute-start | bytes 1044488 | tf_op jit(solution)/shard_map/ppermute | solution.py:28
  107.3 34.2 %collective-permute-start.25 = (bf16[272,640]{1,0:T(8,128)(2,1)}, bf16[272,640]{1,0:T(8,128)(2,1)}, u32[]{:S(2)}, u32[]{:S(2)}) collective-permute-start(bf16[272,640]{1,0:T(8,128)(2,1)} %get-tuple-element.61), channel_id=1, source_target_pairs={{0,6},{2,4},{4,2},{6,0},{1,7},{3,5},{5,3},{7,1},{8,14},{10,12},{12... | collective-permute-start | bytes 1044488 | tf_op jit(solution)/shard_map/ppermute | solution.py:28
  107.3 34.2 %collective-permute-start.24 = (bf16[272,640]{1,0:T(8,128)(2,1)S(1)}, bf16[272,640]{1,0:T(8,128)(2,1)}, u32[]{:S(2)}, u32[]{:S(2)}) collective-permute-start(bf16[272,640]{1,0:T(8,128)(2,1)S(1)} %get-tuple-element.62), channel_id=1, source_target_pairs={{0,4},{2,6},{4,0},{6,2},{1,5},{3,7},{5,1},{7,3},{8,12},{10,14},{12... | collective-permute-start | bytes 1044488 | tf_op jit(solution)/shard_map/ppermute | solution.py:28
  110.8 4.9 %collective-permute-start.32 = (f32[1,1280]{1,0:T(1,128)S(1)}, f32[1,1280]{1,0:T(1,128)S(1)}, u32[]{:S(2)}, u32[]{:S(2)}) collective-permute-start(f32[1,1280]{1,0:T(1,128)S(1)} %fusion.2), channel_id=1, source_target_pairs={{0,64},{32,96},{64,0},{96,32},{128,192},{160,224},{192,128},{224,1... | collective-permute-start | bytes 15368 | tf_op jit(solution)/shard_map/ppermute | solution.py:28
  115.7 7.9 %collective-permute-start.33 = (f32[1,1280]{1,0:T(1,128)S(1)}, f32[1,1280]{1,0:T(1,128)S(1)}, u32[]{:S(2)}, u32[]{:S(2)}) collective-permute-start(f32[1,1280]{1,0:T(1,128)S(1)} %add.165), channel_id=1, source_target_pairs={{0,128},{32,160},{64,192},{96,224},{128,0},{160,32},{192,64},{224,... | collective-permute-start | bytes 15368 | tf_op jit(solution)/shard_map/ppermute | solution.py:28
  123.6 3.7 %collective-permute-start.34 = (f32[1,1280]{1,0:T(1,128)S(1)}, f32[1,1280]{1,0:T(1,128)S(1)}, u32[]{:S(2)}, u32[]{:S(2)}) collective-permute-start(f32[1,1280]{1,0:T(1,128)S(1)} %add.166), channel_id=1, source_target_pairs={{0,8},{8,0},{16,24},{24,16},{1,9},{9,1},{17,25},{25,17},{2,10},{10... | collective-permute-start | bytes 15368 | tf_op jit(solution)/shard_map/ppermute | solution.py:28
  127.3 5.2 %collective-permute-start.35 = (f32[1,1280]{1,0:T(1,128)S(1)}, f32[1,1280]{1,0:T(1,128)S(1)}, u32[]{:S(2)}, u32[]{:S(2)}) collective-permute-start(f32[1,1280]{1,0:T(1,128)S(1)} %add.167), channel_id=1, source_target_pairs={{0,16},{8,24},{16,0},{24,8},{1,17},{9,25},{17,1},{25,9},{2,18},{10... | collective-permute-start | bytes 15368 | tf_op jit(solution)/shard_map/ppermute | solution.py:28
  132.5 5.2 %collective-permute-start.36 = (f32[1,1280]{1,0:T(1,128)S(1)}, f32[1,1280]{1,0:T(1,128)S(1)}, u32[]{:S(2)}, u32[]{:S(2)}) collective-permute-start(f32[1,1280]{1,0:T(1,128)S(1)} %add.168), channel_id=1, source_target_pairs={{0,4},{4,0},{1,5},{5,1},{2,6},{6,2},{3,7},{7,3},{8,12},{12,8},{9,1... | collective-permute-start | bytes 15368 | tf_op jit(solution)/shard_map/ppermute | solution.py:28
  137.7 3.7 %collective-permute-start.37 = (f32[1,640]{1,0:T(1,128)S(1)}, f32[1,640]{1,0:T(1,128)S(1)}, u32[]{:S(2)}, u32[]{:S(2)}) collective-permute-start(f32[1,640]{1,0:T(1,128)S(1)} %slice.62), channel_id=1, source_target_pairs={{0,2},{2,0},{1,3},{3,1},{4,6},{6,4},{5,7},{7,5},{8,10},{10,8},{9,1... | collective-permute-start | bytes 7688 | tf_op jit(solution)/shard_map/ppermute | solution.py:28
  142.9 11.9 %collective-permute-start.26 = (bf16[256,896]{1,0:T(8,128)(2,1)S(1)}, bf16[256,896]{1,0:T(8,128)(2,1)S(1)}, u32[]{:S(2)}, u32[]{:S(2)}) collective-permute-start(bf16[256,896]{1,0:T(8,128)(2,1)S(1)} %slice_bitcast_fusion), channel_id=1, source_target_pairs={{0,4},{4,0},{1,5},{5,1},{2,6},{6,2},{3,7},{7,3},{8,12},{12,8},{9,1... | collective-permute-start | bytes 1376264 | tf_op jit(solution)/shard_map/ppermute | solution.py:28
  150.5 5.6 %collective-permute-start.27 = (bf16[80,896]{1,0:T(8,128)(2,1)S(1)}, bf16[80,896]{1,0:T(8,128)(2,1)S(1)}, u32[]{:S(2)}, u32[]{:S(2)}) collective-permute-start(bf16[80,896]{1,0:T(8,128)(2,1)S(1)} %get-tuple-element.67), channel_id=1, source_target_pairs={{0,8},{8,0},{16,24},{24,16},{1,9},{9,1},{17,25},{25,17},{2,10},{10... | collective-permute-start | bytes 430088 | tf_op jit(solution)/shard_map/ppermute | solution.py:28
  152.0 9.5 %collective-permute-start.29 = (bf16[80,896]{1,0:T(8,128)(2,1)S(1)}, bf16[80,896]{1,0:T(8,128)(2,1)S(1)}, u32[]{:S(2)}, u32[]{:S(2)}) collective-permute-start(bf16[80,896]{1,0:T(8,128)(2,1)S(1)} %get-tuple-element.68), channel_id=1, source_target_pairs={{0,24},{8,16},{16,8},{24,0},{1,25},{9,17},{17,9},{25,1},{2,26},{10... | collective-permute-start | bytes 430088 | tf_op jit(solution)/shard_map/ppermute | solution.py:28
  154.1 7.5 %collective-permute-start.28 = (bf16[80,896]{1,0:T(8,128)(2,1)S(1)}, bf16[80,896]{1,0:T(8,128)(2,1)S(1)}, u32[]{:S(2)}, u32[]{:S(2)}) collective-permute-start(bf16[80,896]{1,0:T(8,128)(2,1)S(1)} %get-tuple-element.69), channel_id=1, source_target_pairs={{0,16},{8,24},{16,0},{24,8},{1,17},{9,25},{17,1},{25,9},{2,18},{10... | collective-permute-start | bytes 430088 | tf_op jit(solution)/shard_map/ppermute | solution.py:28
  162.6 5.9 %collective-permute-start.30 = (bf16[40,896]{1,0:T(8,128)(2,1)S(1)}, bf16[40,896]{1,0:T(8,128)(2,1)S(1)}, u32[]{:S(2)}, u32[]{:S(2)}) collective-permute-start(bf16[40,896]{1,0:T(8,128)(2,1)S(1)} %dynamic-slice_convert_fusion), channel_id=1, source_target_pairs={{0,4},{4,0},{1,5},{5,1},{2,6},{6,2},{3,7},{7,3},{8,12},{12,8},{9,1... | collective-permute-start | bytes 215048 | tf_op jit(solution)/shard_map/ppermute | solution.py:28
  (6 other events, 6.6 us)
Sparse Core Ops, SparseCore 0:
  92.9 56.4 reduce-scatter.1
